TPU v7x, 32 devices: a whole 2x2x4 slice. The times are simulated.
32 devices in a mesh: dp: 8 (over z, x), tensor: 4 (over y, core).
Axes of the slice: x: 2, y: 2, z: 4, core: 2. Of those that a mesh axis runs over, the one named last changes fastest.
Arguments:
- hidden_in: bfloat16 [4096, 768], P(('dp', 'tensor')), may hold values from -6 to 6
- segment_ids: int32 [4096], P('dp'), may hold values from 0 to 1, as said below
- qkv_weight: bfloat16 [2, 768, 3, 768], P(None, 'dp', None, 'tensor'), may hold values from -0.21875 to 0.21875
- qv_bias: float32 [2, 2, 768], P(None, None, 'tensor'), may hold values from -0.12 to 0.12
- out_weight: bfloat16 [2, 768, 768], P(None, 'tensor', 'dp'), may hold values from -3.5 to 3.5
- out_bias: float32 [2, 768], replicated, may hold values from -0.6 to 0.6
- norm_gain: float32 [2, 2, 768], replicated, may hold values from 0.5 to 1.5
- norm_bias: float32 [2, 2, 768], replicated, may hold values from -2 to 2
- up_weight: bfloat16 [2, 768, 3072], P(None, 'dp', 'tensor'), may hold values from -0.21875 to 0.21875
- up_bias: float32 [2, 3072], P(None, 'tensor'), may hold values from -3 to 3
- down_weight: bfloat16 [2, 3072, 768], P(None, 'tensor', 'dp'), may hold values from -0.109375 to 0.109375
- down_bias: float32 [2, 768], replicated, may hold values from -1.2 to 1.2
- out_grad: bfloat16 [4096, 768], P(('dp', 'tensor')), may hold values from -6 to 6
Outputs:
- mixed: bfloat16 [4096, 768], P(('dp', 'tensor'))
- input_grad: float32 [4096, 768], P(('dp', 'tensor'))
- qkv_weight_grad: float32 [2, 768, 3, 768], P(None, 'dp', None, 'tensor')
- qv_bias_grad: float32 [2, 2, 768], P(None, None, 'tensor')
- out_weight_grad: float32 [2, 768, 768], P(None, 'tensor', 'dp')
- out_bias_grad: float32 [2, 768], replicated
- norm_gain_grad: float32 [2, 2, 768], replicated
- norm_bias_grad: float32 [2, 2, 768], replicated
- up_weight_grad: float32 [2, 768, 3072], P(None, 'dp', 'tensor')
- up_bias_grad: float32 [2, 3072], P(None, 'tensor')
- down_weight_grad: float32 [2, 3072, 768], P(None, 'tensor', 'dp')
- down_bias_grad: float32 [2, 768], replicated
Inputs may be any that keep to these rules, and one draw needn't show every extreme that they name: `segment_ids`: each sequence of 512 tokens holds one document (all ids 0) or two (ids 0, then 1), each of the two at least 25 / 64 of 512 tokens long, rounded down; some sequence holds one and some holds two.
All inputs are finite; a program needn't handle non-finite values.
Results may differ from a plain program's by a relative error of at most 0.035.
Values may be sent and summed in bfloat16 or wider, within the bound.
A program may use at most 128 MiB of HBM per device.

v0:
```python
from functools import partial
import math

import jax
import jax.numpy as jnp
from jax import lax
from jax.sharding import PartitionSpec as P

HEAD_DIM = 64
SEQ_LEN = 512


epsilon = 1e-12


def norm_rows(z, gain, shift):
    center = z - jnp.mean(z, axis=-1, keepdims=True)
    spread = jnp.mean(center * center, axis=-1, keepdims=True)
    return center * lax.rsqrt(spread + epsilon) * gain + shift


def gelu_exact(value):
    return jax.nn.gelu(value, approximate=False)


def to_blocks(table, seq_count, head_count):
    total_rows = table.shape[0]
    shaped = table.reshape(seq_count, total_rows // seq_count, head_count, HEAD_DIM)
    return shaped.transpose(0, 2, 1, 3).reshape(
        seq_count * head_count, total_rows // seq_count, HEAD_DIM
    )


def from_blocks(blocks, seq_count, head_count):
    length = blocks.shape[1]
    shaped = blocks.reshape(seq_count, head_count, length, HEAD_DIM)
    return shaped.transpose(0, 2, 1, 3).reshape(seq_count * length, head_count * HEAD_DIM)


def block_scores(query, keys, marks, scale):
    scores = jnp.dot(query, keys.T, preferred_element_type=jnp.float32) * scale
    same = marks[:, None] == marks[None, :]
    return jnp.where(same, scores, -1000000000.0)


def attend_forward(item, scale):
    query, keys, values, marks = item
    scores = block_scores(query, keys, marks, scale)
    totals = jax.nn.logsumexp(scores, axis=-1)
    probs = jnp.exp(scores - totals[:, None])
    attended = jnp.dot(probs.astype(jnp.bfloat16), values, preferred_element_type=jnp.float32)
    return (attended, totals)


def attend_backward(item, scale):
    query, keys, values, marks, totals, grad_heads = item
    scores = block_scores(query, keys, marks, scale)
    probs = jnp.exp(scores - totals[:, None])
    grad_probs = jnp.dot(grad_heads, values.T, preferred_element_type=jnp.float32)
    inner = jnp.sum(probs * grad_probs, axis=-1, keepdims=True)
    grad_scores = (probs * (grad_probs - inner)).astype(jnp.bfloat16)
    grad_query = jnp.dot(grad_scores, keys, preferred_element_type=jnp.float32) * scale
    grad_keys = jnp.dot(grad_scores.T, query, preferred_element_type=jnp.float32) * scale
    grad_values = jnp.dot(
        probs.astype(jnp.bfloat16).T, grad_heads, preferred_element_type=jnp.float32
    )
    return (grad_query, grad_keys, grad_values)


def per_device(
    hidden_in,
    segment_ids,
    qkv_weight,
    qv_bias,
    out_weight,
    out_bias,
    norm_gain,
    norm_bias,
    up_weight,
    up_bias,
    down_weight,
    down_bias,
    out_grad,
):
    layers = qkv_weight.shape[0]
    width = out_bias.shape[1]
    total_rows = segment_ids.shape[0]
    seq_count = total_rows // SEQ_LEN
    head_count = qv_bias.shape[2] // HEAD_DIM
    scale = 1.0 / math.sqrt(HEAD_DIM)
    marks = jnp.broadcast_to(
        segment_ids.reshape(seq_count, 1, SEQ_LEN), (seq_count, head_count, SEQ_LEN)
    ).reshape(seq_count * head_count, SEQ_LEN)

    def fetch(depth):
        return (
            lax.all_gather(qkv_weight[depth], "dp", axis=0, tiled=True),
            lax.all_gather(out_weight[depth], "dp", axis=1, tiled=True),
            lax.all_gather(up_weight[depth], "dp", axis=0, tiled=True),
            lax.all_gather(down_weight[depth], "dp", axis=1, tiled=True),
        )

    rows = hidden_in.astype(jnp.float32)
    kept = []
    gathered = []
    for depth in range(layers):
        joint_weight, merge_weight, lift_weight, drop_weight = fetch(depth)
        gathered.append((joint_weight, merge_weight, lift_weight, drop_weight))
        joint_flat = joint_weight.reshape(width, -1)
        inputs = lax.all_gather(rows.astype(jnp.bfloat16), "tensor", axis=0, tiled=True)
        projected = jnp.dot(inputs, joint_flat, preferred_element_type=jnp.float32).reshape(
            total_rows, 3, -1
        )
        query = (projected[:, 0] + qv_bias[depth, 0]).astype(jnp.bfloat16)
        keys = projected[:, 1].astype(jnp.bfloat16)
        values = (projected[:, 2] + qv_bias[depth, 1]).astype(jnp.bfloat16)
        query_blocks = to_blocks(query, seq_count, head_count)
        key_blocks = to_blocks(keys, seq_count, head_count)
        value_blocks = to_blocks(values, seq_count, head_count)
        attended, totals = lax.map(
            partial(attend_forward, scale=scale), (query_blocks, key_blocks, value_blocks, marks)
        )
        heads_out = from_blocks(attended, seq_count, head_count).astype(jnp.bfloat16)
        attn_term = jnp.dot(heads_out, merge_weight, preferred_element_type=jnp.float32)
        branch = (
            lax.psum_scatter(
                attn_term.astype(jnp.bfloat16), "tensor", scatter_dimension=0, tiled=True
            ).astype(jnp.float32)
            + out_bias[depth]
        )
        first_in = rows + branch
        first = norm_rows(first_in, norm_gain[depth, 0], norm_bias[depth, 0])
        middle = lax.all_gather(first.astype(jnp.bfloat16), "tensor", axis=0, tiled=True)
        hidden_pre = (
            jnp.dot(middle, lift_weight, preferred_element_type=jnp.float32) + up_bias[depth]
        )
        hidden = gelu_exact(hidden_pre).astype(jnp.bfloat16)
        ffn_term = jnp.dot(hidden, drop_weight, preferred_element_type=jnp.float32)
        second_in = first + (
            lax.psum_scatter(
                ffn_term.astype(jnp.bfloat16), "tensor", scatter_dimension=0, tiled=True
            ).astype(jnp.float32)
            + down_bias[depth]
        )
        kept.append(
            (
                rows,
                inputs,
                query_blocks,
                key_blocks,
                value_blocks,
                totals,
                heads_out,
                first_in,
                middle,
                hidden_pre,
                hidden,
                second_in,
            )
        )
        rows = norm_rows(second_in, norm_gain[depth, 1], norm_bias[depth, 1])
    mixed = rows.astype(jnp.bfloat16)
    grad = out_grad.astype(jnp.float32)
    weight_parts = [None] * layers
    split_parts = [None] * layers
    shared_parts = [None] * layers
    for depth in reversed(range(layers)):
        (
            rows_in,
            inputs,
            query_blocks,
            key_blocks,
            value_blocks,
            totals,
            heads_out,
            first_in,
            middle,
            hidden_pre,
            hidden,
            second_in,
        ) = kept[depth]
        joint_weight, merge_weight, lift_weight, drop_weight = fetch(depth)
        joint_flat = joint_weight.reshape(width, -1)
        unused, norm_pull = jax.vjp(norm_rows, second_in, norm_gain[depth, 1], norm_bias[depth, 1])
        grad_second, gain_two, shift_two = norm_pull(grad)
        grad_ffn = grad_second.astype(jnp.bfloat16)
        drop_bias_grad = jnp.sum(grad_ffn.astype(jnp.float32), axis=0)
        grad_ffn_full = lax.all_gather(grad_ffn, "tensor", axis=0, tiled=True)
        drop_grad = jnp.dot(grad_ffn_full.T, hidden, preferred_element_type=jnp.float32)
        grad_hidden = jnp.dot(grad_ffn_full, drop_weight.T, preferred_element_type=jnp.float32)
        unused, gelu_pull = jax.vjp(gelu_exact, hidden_pre)
        grad_pre = gelu_pull(grad_hidden)[0].astype(jnp.bfloat16)
        lift_bias_grad = jnp.sum(grad_pre.astype(jnp.float32), axis=0)
        lift_grad = jnp.dot(middle.T, grad_pre, preferred_element_type=jnp.float32)
        lift_term = jnp.dot(grad_pre, lift_weight.T, preferred_element_type=jnp.float32)
        grad_first = grad_second + lax.psum_scatter(
            lift_term.astype(jnp.bfloat16), "tensor", scatter_dimension=0, tiled=True
        ).astype(jnp.float32)
        unused, norm_pull = jax.vjp(norm_rows, first_in, norm_gain[depth, 0], norm_bias[depth, 0])
        grad_first_in, gain_one, shift_one = norm_pull(grad_first)
        grad_branch = grad_first_in.astype(jnp.bfloat16)
        merge_bias_grad = jnp.sum(grad_branch.astype(jnp.float32), axis=0)
        grad_branch_full = lax.all_gather(grad_branch, "tensor", axis=0, tiled=True)
        merge_grad = jnp.dot(grad_branch_full.T, heads_out, preferred_element_type=jnp.float32)
        grad_heads = jnp.dot(
            grad_branch_full, merge_weight.T, preferred_element_type=jnp.float32
        ).astype(jnp.bfloat16)
        grad_query, grad_keys, grad_values = lax.map(
            partial(attend_backward, scale=scale),
            (
                query_blocks,
                key_blocks,
                value_blocks,
                marks,
                totals,
                to_blocks(grad_heads, seq_count, head_count),
            ),
        )
        grad_joint = jnp.stack(
            [
                from_blocks(grad_query, seq_count, head_count),
                from_blocks(grad_keys, seq_count, head_count),
                from_blocks(grad_values, seq_count, head_count),
            ],
            axis=1,
        ).astype(jnp.bfloat16)
        pair_bias_grad = jnp.sum(grad_joint[:, 0::2].astype(jnp.float32), axis=0)
        grad_flat = grad_joint.reshape(total_rows, -1)
        joint_grad = jnp.dot(inputs.T, grad_flat, preferred_element_type=jnp.float32).reshape(
            width, 3, -1
        )
        joint_term = jnp.dot(grad_flat, joint_flat.T, preferred_element_type=jnp.float32)
        grad = grad_first_in + lax.psum_scatter(
            joint_term.astype(jnp.bfloat16), "tensor", scatter_dimension=0, tiled=True
        ).astype(jnp.float32)
        weight_parts[depth] = (
            lax.psum_scatter(joint_grad, "dp", scatter_dimension=0, tiled=True),
            lax.psum_scatter(merge_grad, "dp", scatter_dimension=0, tiled=True),
            lax.psum_scatter(lift_grad, "dp", scatter_dimension=0, tiled=True),
            lax.psum_scatter(drop_grad, "dp", scatter_dimension=0, tiled=True),
        )
        split_parts[depth] = (pair_bias_grad, lift_bias_grad)
        shared_parts[depth] = (
            merge_bias_grad,
            jnp.stack([gain_one, gain_two]),
            jnp.stack([shift_one, shift_two]),
            drop_bias_grad,
        )
    stacks = [
        jnp.stack([weight_parts[depth][index] for depth in range(layers)]) for index in range(4)
    ]
    merge_total = jnp.transpose(stacks[1], (0, 2, 1))
    drop_total = jnp.transpose(stacks[3], (0, 2, 1))
    pair_stack = jnp.stack([split_parts[depth][0] for depth in range(layers)])
    lift_bias_stack = jnp.stack([split_parts[depth][1] for depth in range(layers)])
    pair_total, lift_bias_total = lax.psum((pair_stack, lift_bias_stack), "dp")
    merge_bias_stack = jnp.stack([shared_parts[depth][0] for depth in range(layers)])
    gain_stack = jnp.stack([shared_parts[depth][1] for depth in range(layers)])
    shift_stack = jnp.stack([shared_parts[depth][2] for depth in range(layers)])
    drop_bias_stack = jnp.stack([shared_parts[depth][3] for depth in range(layers)])
    merge_bias_total, gain_total, shift_total, drop_bias_total = lax.psum(
        (merge_bias_stack, gain_stack, shift_stack, drop_bias_stack), ("dp", "tensor")
    )
    return (
        mixed,
        grad,
        stacks[0],
        pair_total,
        merge_total,
        merge_bias_total,
        gain_total,
        shift_total,
        stacks[2],
        lift_bias_total,
        drop_total,
        drop_bias_total,
    )


def solution(mesh):
    in_specs = (
        P(("dp", "tensor"), None),
        P("dp"),
        P(None, "dp", None, "tensor"),
        P(None, None, "tensor"),
        P(None, "tensor", "dp"),
        P(),
        P(),
        P(),
        P(None, "dp", "tensor"),
        P(None, "tensor"),
        P(None, "tensor", "dp"),
        P(),
        P(("dp", "tensor"), None),
    )
    out_specs = (
        P(("dp", "tensor"), None),
        P(("dp", "tensor"), None),
        P(None, "dp", None, "tensor"),
        P(None, None, "tensor"),
        P(None, "tensor", "dp"),
        P(),
        P(),
        P(),
        P(None, "dp", "tensor"),
        P(None, "tensor"),
        P(None, "tensor", "dp"),
        P(),
    )
    return jax.shard_map(
        per_device, mesh=mesh, in_specs=in_specs, out_specs=out_specs, check_vma=False
    )
```

profile of v0, /device:TPU:0, one launch (start us, length us, event | category | flops | bytes accessed | tf_op | source)
XLA Modules:
  0.0 1138.4 jit_solution(12218449914813924439)
XLA Ops:
  9.2 10.3 all_gather.56
  19.5 38.0 %all-gather = bf16[1,768,3,192]{3,2,0,1:T(4,128)(2,1)S(1)} all-gather(bf16[1,96,3,192]{3,2,0,1:T(4,128)(2,1)S(1)} %copy.80), channel_id=2, replica_groups=mesh['dp'=8,'tensor'=4] {'dp'}, dimensions={1}, use_global_device_ids=true | all-gather | bytes 995328 | tf_op jit(solution)/shard_map/all_gather | solution.py:97
  62.4 32.1 %all-gather.1 = bf16[1,192,768]{1,0,2:T(2,128)(2,1)S(1)} all-gather(bf16[1,192,96]{1,0,2:T(2,128)(2,1)S(1)} %copy.81), channel_id=3, replica_groups=mesh['dp'=8,'tensor'=4] {'dp'}, dimensions={2}, use_global_device_ids=true | all-gather | bytes 331776 | tf_op jit(solution)/shard_map/all_gather | solution.py:98
  104.6 17.9 %reduce-scatter.17.cloned.1.call-done = bf16[128,768]{1,0:T(8,128)(2,1)} async-done(((bf16[512,768]{1,0:T(8,128)(2,1)}), bf16[128,768]{1,0:T(8,128)(2,1)}) %reduce-scatter.17.cloned.1.call-update) | async-done | bytes 196624 | tf_op jit(solution)/shard_map/reduce_scatter | solution.py:126
  150.5 36.5 %all-gather.15.cloned.1.call-done = bf16[1,768,768]{1,2,0:T(8,128)(2,1)} async-done(((bf16[1,768,96]{1,2,0:T(8,128)(2,1)}), bf16[1,768,768]{1,2,0:T(8,128)(2,1)}) %all-gather.15.cloned.1.call-update) | async-done | bytes 1179664 | tf_op jit(solution)/shard_map/all_gather | solution.py:100
  191.6 32.0 %all-gather.5 = bf16[1,192,768]{1,0,2:T(2,128)(2,1)S(1)} all-gather(bf16[1,192,96]{1,0,2:T(2,128)(2,1)S(1)} %copy.83), channel_id=7, replica_groups=mesh['dp'=8,'tensor'=4] {'dp'}, dimensions={2}, use_global_device_ids=true | all-gather | bytes 331776 | tf_op jit(solution)/shard_map/all_gather | solution.py:98
  225.2 35.8 %all-gather.4 = bf16[1,768,3,192]{3,2,0,1:T(4,128)(2,1)S(1)} all-gather(bf16[1,96,3,192]{3,2,0,1:T(4,128)(2,1)S(1)} %copy.82), channel_id=6, replica_groups=mesh['dp'=8,'tensor'=4] {'dp'}, dimensions={1}, use_global_device_ids=true | all-gather | bytes 995328 | tf_op jit(solution)/shard_map/all_gather | solution.py:97
  290.7 19.7 %reduce-scatter.21.cloned.1.call-done = bf16[128,768]{1,0:T(8,128)(2,1)} async-done(((bf16[512,768]{1,0:T(8,128)(2,1)}), bf16[128,768]{1,0:T(8,128)(2,1)}) %reduce-scatter.21.cloned.1.call-update) | async-done | bytes 196624 | tf_op jit(solution)/shard_map/reduce_scatter | solution.py:126
  321.8 10.1 all-gather.17.cloned.1.call-done
  339.1 35.8 %all-gather.19.cloned.1.call-done = bf16[1,768,768]{1,2,0:T(8,128)(2,1)} async-done(((bf16[1,768,96]{1,2,0:T(8,128)(2,1)}), bf16[1,768,768]{1,2,0:T(8,128)(2,1)}) %all-gather.19.cloned.1.call-update) | async-done | bytes 1179664 | tf_op jit(solution)/shard_map/all_gather | solution.py:100
  378.3 21.9 %reduce-scatter.23.cloned.1.call-done = bf16[128,768]{1,0:T(8,128)(2,1)} async-done(((bf16[512,768]{1,0:T(8,128)(2,1)}), bf16[128,768]{1,0:T(8,128)(2,1)}) %reduce-scatter.23.cloned.1.call-update) | async-done | bytes 196624 | tf_op jit(solution)/shard_map/reduce_scatter | solution.py:140
  418.7 23.8 %reduce-scatter.25.cloned.1.call-done = bf16[128,768]{1,0:T(8,128)(2,1)} async-done(((bf16[512,768]{1,0:T(8,128)(2,1)}), bf16[128,768]{1,0:T(8,128)(2,1)}) %reduce-scatter.25.cloned.1.call-update) | async-done | bytes 196624 | tf_op jit(solution)/shard_map/reduce_scatter | solution.py:196
  459.8 14.1 %while.54 = (s32[]{:T(128)}, bf16[3,512,64]{1,2,0:T(8,128)(2,1)}, bf16[3,512,64]{1,2,0:T(8,128)(2,1)}, bf16[3,512,64]{1,2,0:T(8,128)(2,1)}, s32[3,512]{1,0:T(4,1...) while((s32[]{:T(128)}, bf16[3,512,64]{1,2,0:T(8,128)(2,1)}, ...), condition=%wide.region_27.28_spmd, body=%wide.region_25.27_spmd.sunk | while | flops 170458624 | bytes 13917477 | solution.py:208
  477.4 23.6 %reduce-scatter.27.cloned.1.call-done = bf16[128,768]{1,0:T(8,128)(2,1)} async-done(((bf16[512,768]{1,0:T(8,128)(2,1)}), bf16[128,768]{1,0:T(8,128)(2,1)}) %reduce-scatter.27.cloned.1.call-update) | async-done | bytes 196624 | tf_op jit(solution)/shard_map/reduce_scatter | solution.py:233
  520.7 22.3 %reduce-scatter.29.cloned.1.call-done = bf16[128,768]{1,0:T(8,128)(2,1)} async-done(((bf16[512,768]{1,0:T(8,128)(2,1)}), bf16[128,768]{1,0:T(8,128)(2,1)}) %reduce-scatter.29.cloned.1.call-update) | async-done | bytes 196624 | tf_op jit(solution)/shard_map/reduce_scatter | solution.py:196
  589.9 37.1 %all-reduce.1 = (f32[2,2,192]{2,1,0:T(2,128)}, f32[2,768]{1,0:T(2,128)}) all-reduce(f32[2,2,192]{2,1,0:T(2,128)S(1)} %pad_maximum_fusion.7, f32[2,768]{1,0:T(2,128)S(1)} %pad_maximum_fusion.5), channel_id=1, replica_groups=mesh['dp'=8,'tensor'=4] {'dp'}, use_global_device_ids=true, to_apply=%region_42.43 | all-reduce | flops 2304 | bytes 18432 | tf_op jit(solution)/shard_map/psum | solution.py:256
  627.1 38.0 %all-reduce = (f32[2,768]{1,0:T(2,128)}, f32[2,2,768]{2,1,0:T(2,128)}, f32[2,2,768]{2,1,0:T(2,128)}, f32[2,768]{1,0:T(2,128)}) all-reduce(f32[2,768]{1,0:T(2,128)S(1)} %pad_maximum_fusion.4, f32[2,2,768]{2,1,0:T(2,128)S(1)} %pad_maximum_fusion.2, ...), channel_id=1, replica_groups=mesh['dp'=8,'tensor'=4] {'dp','tensor'}, use_global_device_ids=true, to_apply=%region_47.48 | all-reduce | flops 9216 | bytes 73728 | tf_op jit(solution)/shard_map/psum | solution.py:261
  676.0 23.0 %reduce-scatter.31.cloned.1.call-done = bf16[128,768]{1,0:T(8,128)(2,1)} async-done(((bf16[512,768]{1,0:T(8,128)(2,1)}), bf16[128,768]{1,0:T(8,128)(2,1)}) %reduce-scatter.31.cloned.1.call-update) | async-done | bytes 196624 | tf_op jit(solution)/shard_map/reduce_scatter | solution.py:233
  700.8 71.1 %reduce-scatter.47.cloned.1.call-done = f32[96,768]{1,0:T(8,128)} async-done(((f32[768,768]{1,0:T(8,128)}), f32[96,768]{1,0:T(8,128)}) %reduce-scatter.47.cloned.1.call-update) | async-done | bytes 294928 | tf_op jit(solution)/shard_map/reduce_scatter | solution.py:240
  771.9 71.3 %reduce-scatter.45.cloned.1.call-done = f32[96,768]{1,0:T(8,128)} async-done(((f32[768,768]{1,0:T(8,128)}), f32[96,768]{1,0:T(8,128)}) %reduce-scatter.45.cloned.1.call-update) | async-done | bytes 294928 | tf_op jit(solution)/shard_map/reduce_scatter | solution.py:240
  845.1 69.6 %reduce-scatter.43.cloned.1.call-done = f32[96,768]{1,0:T(8,128)} async-done(((f32[768,768]{1,0:T(8,128)}), f32[96,768]{1,0:T(8,128)}) %reduce-scatter.43.cloned.1.call-update) | async-done | bytes 294928 | tf_op jit(solution)/shard_map/reduce_scatter | solution.py:239
  914.7 71.4 %reduce-scatter.41.cloned.1.call-done = f32[96,768]{1,0:T(8,128)} async-done(((f32[768,768]{1,0:T(8,128)}), f32[96,768]{1,0:T(8,128)}) %reduce-scatter.41.cloned.1.call-update) | async-done | bytes 294928 | tf_op jit(solution)/shard_map/reduce_scatter | solution.py:239
  988.0 69.3 %reduce-scatter.35.cloned.1.call-done = f32[96,3,192]{2,0,1:T(8,128)} async-done(((f32[768,3,192]{2,0,1:T(8,128)}), f32[96,3,192]{2,0,1:T(8,128)}) %reduce-scatter.35.cloned.1.call-update) | async-done | bytes 221200 | tf_op jit(solution)/shard_map/reduce_scatter | solution.py:237
  1057.3 71.4 %reduce-scatter.33.cloned.1.call-done = f32[96,3,192]{2,0,1:T(8,128)} async-done(((f32[768,3,192]{2,0,1:T(8,128)}), f32[96,3,192]{2,0,1:T(8,128)}) %reduce-scatter.33.cloned.1.call-update) | async-done | bytes 221200 | tf_op jit(solution)/shard_map/reduce_scatter | solution.py:237
  (540 shorter events, 255.1 us)
Async XLA Ops:
  8.0 114.5 %reduce-scatter.17.cloned.1.call-start = ((), (), s32[]{:S(2)}) async-start(), calls=%async_computation.16 | async-start | bytes 983040 | tf_op jit(solution)/shard_map/reduce_scatter | solution.py:126
  100.4 43.6 %all-gather.13.cloned.1.call-start = ((), (), s32[]{:S(2)}) async-start(), calls=%async_computation.32 | async-start | bytes 1327104 | tf_op jit(solution)/shard_map/all_gather | solution.py:99
  101.3 85.7 %all-gather.15.cloned.1.call-start = ((), (), s32[]{:S(2)}) async-start(), calls=%async_computation.33 | async-start | bytes 1327104 | tf_op jit(solution)/shard_map/all_gather | solution.py:100
  102.1 161.6 %reduce-scatter.19.cloned.1.call-start = ((), (), s32[]{:S(2)}) async-start(), calls=%async_computation.17 | async-start | bytes 983040 | tf_op jit(solution)/shard_map/reduce_scatter | solution.py:140
  104.0 161.1 %copy-start.53 = (f32[768]{0:T(1024)}, f32[768]{0:T(1024)S(1)}, u32[]{:S(2)}) copy-start(f32[768]{0:T(1024)S(1)} %get-tuple-element.255) | copy-start | bytes 9220
  104.6 160.5 %copy-start.59 = (f32[768]{0:T(1024)}, f32[768]{0:T(1024)S(1)}, u32[]{:S(2)}) copy-start(f32[768]{0:T(1024)S(1)} %get-tuple-element.259) | copy-start | bytes 9220
  123.6 140.1 %copy-start.72 = (f32[128]{0:T(128)}, f32[128]{0:T(128)S(1)}, u32[]{:S(2)}) copy-start(f32[128]{0:T(128)S(1)} %broadcast_multiply_fusion.3) | copy-start | bytes 1540
  124.8 139.0 %copy-start.79 = (f32[128]{0:T(128)}, f32[128]{0:T(128)S(1)}, u32[]{:S(2)}) copy-start(f32[128]{0:T(128)S(1)} %fusion.138) | copy-start | bytes 1540
  190.0 120.4 %reduce-scatter.21.cloned.1.call-start = ((), (), s32[]{:S(2)}) async-start(), calls=%async_computation.18 | async-start | bytes 983040 | tf_op jit(solution)/shard_map/reduce_scatter | solution.py:126
  289.1 42.8 %all-gather.17.cloned.1.call-start = ((), (), s32[]{:S(2)}) async-start(), calls=%async_computation.34 | async-start | bytes 1327104 | tf_op jit(solution)/shard_map/all_gather | solution.py:99
  289.7 85.3 %all-gather.19.cloned.1.call-start = ((), (), s32[]{:S(2)}) async-start(), calls=%async_computation.35 | async-start | bytes 1327104 | tf_op jit(solution)/shard_map/all_gather | solution.py:100
  290.4 109.7 %reduce-scatter.23.cloned.1.call-start = ((), (), s32[]{:S(2)}) async-start(), calls=%async_computation.19 | async-start | bytes 983040 | tf_op jit(solution)/shard_map/reduce_scatter | solution.py:140
  378.2 64.3 %reduce-scatter.25.cloned.1.call-start = ((), (), s32[]{:S(2)}) async-start(), calls=%async_computation.20 | async-start | bytes 983040 | tf_op jit(solution)/shard_map/reduce_scatter | solution.py:196
  418.7 82.3 %reduce-scatter.27.cloned.1.call-start = ((), (), s32[]{:S(2)}) async-start(), calls=%async_computation.21 | async-start | bytes 983040 | tf_op jit(solution)/shard_map/reduce_scatter | solution.py:233
  477.2 65.9 %reduce-scatter.29.cloned.1.call-start = ((), (), s32[]{:S(2)}) async-start(), calls=%async_computation.22 | async-start | bytes 983040 | tf_op jit(solution)/shard_map/reduce_scatter | solution.py:196
  519.3 145.9 %reduce-scatter.39.cloned.1.call-start = ((), (), s32[]{:S(2)}) async-start(), calls=%async_computation.27 | async-start | bytes 884736 | tf_op jit(solution)/shard_map/reduce_scatter | solution.py:238
  520.7 153.5 %reduce-scatter.37.cloned.1.call-start = ((), (), s32[]{:S(2)}) async-start(), calls=%async_computation.26 | async-start | bytes 884736 | tf_op jit(solution)/shard_map/reduce_scatter | solution.py:238
  556.6 142.3 %reduce-scatter.31.cloned.1.call-start = ((), (), s32[]{:S(2)}) async-start(), calls=%async_computation.23 | async-start | bytes 983040 | tf_op jit(solution)/shard_map/reduce_scatter | solution.py:233
  566.5 205.4 %reduce-scatter.47.cloned.1.call-start = ((), (), s32[]{:S(2)}) async-start(), calls=%async_computation.31 | async-start | bytes 2654208 | tf_op jit(solution)/shard_map/reduce_scatter | solution.py:240
  569.9 273.3 %reduce-scatter.45.cloned.1.call-start = ((), (), s32[]{:S(2)}) async-start(), calls=%async_computation.30 | async-start | bytes 2654208 | tf_op jit(solution)/shard_map/reduce_scatter | solution.py:240
  573.5 341.2 %reduce-scatter.43.cloned.1.call-start = ((), (), s32[]{:S(2)}) async-start(), calls=%async_computation.29 | async-start | bytes 2654208 | tf_op jit(solution)/shard_map/reduce_scatter | solution.py:239
  577.2 409.0 %reduce-scatter.41.cloned.1.call-start = ((), (), s32[]{:S(2)}) async-start(), calls=%async_computation.28 | async-start | bytes 2654208 | tf_op jit(solution)/shard_map/reduce_scatter | solution.py:239
  580.7 476.6 %reduce-scatter.35.cloned.1.call-start = ((), (), s32[]{:S(2)}) async-start(), calls=%async_computation.25 | async-start | bytes 2654208 | tf_op jit(solution)/shard_map/reduce_scatter | solution.py:237
  584.3 544.4 %reduce-scatter.33.cloned.1.call-start = ((), (), s32[]{:S(2)}) async-start(), calls=%async_computation.24 | async-start | bytes 2654208 | tf_op jit(solution)/shard_map/reduce_scatter | solution.py:237
  (118 other events, 684.3 us)
Sparse Core Ops, SparseCore 0:
  100.6 21.9 reduce-scatter.16
  190.1 21.7 reduce-scatter.18
  289.2 21.1 reduce-scatter.20
  378.3 21.7 reduce-scatter.22
  418.8 23.6 reduce-scatter.24
  477.3 23.6 reduce-scatter.26
  519.4 23.6 reduce-scatter.28
  546.7 62.6 reduce-scatter.38
  612.7 61.4 reduce-scatter.36
  676.7 22.2 reduce-scatter.30
  702.5 69.3 reduce-scatter.46
  775.2 67.9 reduce-scatter.44
  846.7 67.9 reduce-scatter.42
  918.1 68.0 reduce-scatter.40
  989.5 67.8 reduce-scatter.34
  1060.7 68.0 reduce-scatter.32
Sparse Core Ops, SparseCore 1:
  103.9 40.1 all-gather.12
  146.9 40.0 all-gather.14
  292.6 39.3 all-gather.16
  335.0 40.0 all-gather.18
where the time goes:
time: 1150 us; the launch traced here: 1140 us
  waiting for transfers between devices  679 us (59%)
  blocking collectives  282 us (25%)
  matrix products  69.8 us (6%)
  local copies, waits for them, and re-layouts  50.8 us (4%)
  other arithmetic  37.4 us (3%)
  between operations  17.3 us (2%)
    reduce_scatter x2, waiting for transfers between devices, per_device(): lax.psum_scatter(drop_grad, 'dp', scatter_dimension=0, tiled=True)  142 us
    reduce_scatter x2, waiting for transfers between devices, per_device(): lax.psum_scatter(lift_grad, 'dp', scatter_dimension=0, tiled=True)  141 us
    reduce_scatter x2, waiting for transfers between devices, per_device(): lax.psum_scatter(joint_grad, 'dp', scatter_dimension=0, tiled=True)  141 us
    all_gather x2, blocking collectives, fetch(): lax.all_gather(qkv_weight[depth], 'dp', axis=0, tiled=True)  73.8 us
    all_gather x2, waiting for transfers between devices, fetch(): lax.all_gather(down_weight[depth], 'dp', axis=1, tiled=True)  72.3 us
    all_gather x2, blocking collectives, fetch(): lax.all_gather(out_weight[depth], 'dp', axis=1, tiled=True)  64.1 us
    reduce_scatter x2, waiting for transfers between devices, per_device(): lax.psum_scatter(joint_term.astype(jnp.bfloat16), 'tensor', scatter_dimen...  46.6 us
    reduce_scatter x2, waiting for transfers between devices, per_device(): lax.psum_scatter(lift_term.astype(jnp.bfloat16), 'tensor', scatter_dimens...  46.1 us
  transfers between devices with their start and end apart: 20, of which 18 were waited for; matrix products, arithmetic and copies ran while one was open for 6% of the time, Pallas kernels for 0%

commit v1 on v0

--- a/solution.py
+++ b/solution.py
@@ -67,7 +67,93 @@
     return (grad_query, grad_keys, grad_values)
 
 
+def swap(block, axis, bit, size):
+    return lax.ppermute(block, axis, [(i, i ^ bit) for i in range(size)])
+
+
+def ring(block):
+    return lax.ppermute(block, "dp", [(i, (i + 2) % 8) for i in range(8)])
+
+
+def gather_rows(shard, dp_size):
+    pieces, count, cols = shard.shape
+    if dp_size != 8:
+        return lax.all_gather(shard, "dp", axis=1, tiled=True)
+    me = lax.axis_index("dp")
+    far, near = me // 2, me % 2
+    whole = jnp.zeros((pieces, 4, 2, count, cols), shard.dtype)
+    held = shard
+    for step in range(4):
+        place = (far - step) % 4
+        other = swap(held, "dp", 1, 8)
+        for side, block in ((near, held), (1 - near, other)):
+            whole = lax.dynamic_update_slice(
+                whole, block[:, None, None], (0, place, side, 0, 0)
+            )
+        if step < 3:
+            held = ring(held)
+    return whole.reshape(pieces, 8 * count, cols)
+
+
+def scatter_rows(total, dp_size):
+    if dp_size != 8:
+        return lax.psum_scatter(total, "dp", scatter_dimension=1, tiled=True)
+    pieces, rows, cols = total.shape
+    me = lax.axis_index("dp")
+    far, near = me // 2, me % 2
+    parts = total.reshape(pieces, 4, 2, rows // 8, cols)
+    away = lax.dynamic_index_in_dim(parts, 1 - near, 2, keepdims=False)
+    home = lax.dynamic_index_in_dim(parts, near, 2, keepdims=False)
+    here = []
+    for step in range(4):
+        place = (far - 1 - step) % 4
+        sent = lax.dynamic_index_in_dim(away, place, 1, keepdims=False)
+        kept = lax.dynamic_index_in_dim(home, place, 1, keepdims=False)
+        came = swap(sent.astype(jnp.bfloat16), "dp", 1, 8)
+        here.append(kept.astype(jnp.float32) + came.astype(jnp.float32))
+    summed = here[0]
+    for step in range(1, 4):
+        summed = ring(summed.astype(jnp.bfloat16)).astype(jnp.float32) + here[step]
+    return summed
+
+
+def scatter_tokens(term):
+    rows, width = term.shape
+    me = lax.axis_index("tensor")
+    far, near = me // 2, me % 2
+    parts = term.reshape(2, 2, rows // 4, width)
+    away = lax.dynamic_index_in_dim(parts, 1 - near, 1, keepdims=False)
+    home = lax.dynamic_index_in_dim(parts, near, 1, keepdims=False)
+    pair = home.astype(jnp.float32) + swap(
+        away.astype(jnp.bfloat16), "tensor", 1, 4
+    ).astype(jnp.float32)
+    away = lax.dynamic_index_in_dim(pair, 1 - far, 0, keepdims=False)
+    home = lax.dynamic_index_in_dim(pair, far, 0, keepdims=False)
+    return home + swap(away.astype(jnp.bfloat16), "tensor", 2, 4).astype(jnp.float32)
+
+
+def sum_small(shared, split, dp_size):
+    joined = jnp.concatenate([shared, split]).reshape(-1, 128)
+    if dp_size != 8:
+        joined = lax.psum(joined, "dp")
+    else:
+        for bit in (1, 2, 4):
+            joined = joined + swap(joined, "dp", bit, 8)
+    cut = shared.shape[0] // 128
+    shared = joined[:cut]
+    for bit in (1, 2):
+        shared = shared + swap(shared, "tensor", bit, 4)
+    return shared.reshape(-1), joined[cut:].reshape(-1)
+
+
+def dot_nt(left, right):
+    return lax.dot_general(
+        left, right, (((1,), (1,)), ((), ())), preferred_element_type=jnp.float32
+    )
+
+
 def per_device(
+    dp_count,
     hidden_in,
     segment_ids,
     qkv_weight,
@@ -92,21 +178,30 @@
         segment_ids.reshape(seq_count, 1, SEQ_LEN), (seq_count, head_count, SEQ_LEN)
     ).reshape(seq_count * head_count, SEQ_LEN)
 
-    def fetch(depth):
-        return (
-            lax.all_gather(qkv_weight[depth], "dp", axis=0, tiled=True),
-            lax.all_gather(out_weight[depth], "dp", axis=1, tiled=True),
-            lax.all_gather(up_weight[depth], "dp", axis=0, tiled=True),
-            lax.all_gather(down_weight[depth], "dp", axis=1, tiled=True),
-        )
+    dp_size = dp_count
+    joint_cols = qkv_weight.shape[2] * qkv_weight.shape[3]
+    shards = []
+    for depth in range(layers):
+        joint_shard = jnp.concatenate(
+            [qkv_weight[depth].reshape(-1, joint_cols), out_weight[depth].T], axis=1
+        )
+        lift_shard = jnp.stack([up_weight[depth], down_weight[depth].T])
+        shards.append((joint_shard[None], lift_shard))
 
     rows = hidden_in.astype(jnp.float32)
     kept = []
     gathered = []
     for depth in range(layers):
-        joint_weight, merge_weight, lift_weight, drop_weight = fetch(depth)
-        gathered.append((joint_weight, merge_weight, lift_weight, drop_weight))
-        joint_flat = joint_weight.reshape(width, -1)
+        joint_shard, lift_shard = shards[depth]
+        if depth > 0:
+            joint_shard, lift_shard, unused = lax.optimization_barrier(
+                (joint_shard, lift_shard, gathered[depth - 1][0])
+            )
+        joint_all = gather_rows(joint_shard, dp_size)[0]
+        lift_all = gather_rows(lift_shard, dp_size)
+        joint_flat, merge_flat = joint_all[:, :joint_cols], joint_all[:, joint_cols:]
+        lift_weight, drop_flat = lift_all[0], lift_all[1]
+        gathered.append((lift_all, joint_flat, merge_flat, lift_weight, drop_flat))
         inputs = lax.all_gather(rows.astype(jnp.bfloat16), "tensor", axis=0, tiled=True)
         projected = jnp.dot(inputs, joint_flat, preferred_element_type=jnp.float32).reshape(
             total_rows, 3, -1
@@ -121,11 +216,9 @@
             partial(attend_forward, scale=scale), (query_blocks, key_blocks, value_blocks, marks)
         )
         heads_out = from_blocks(attended, seq_count, head_count).astype(jnp.bfloat16)
-        attn_term = jnp.dot(heads_out, merge_weight, preferred_element_type=jnp.float32)
+        attn_term = dot_nt(heads_out, merge_flat)
         branch = (
-            lax.psum_scatter(
-                attn_term.astype(jnp.bfloat16), "tensor", scatter_dimension=0, tiled=True
-            ).astype(jnp.float32)
+            scatter_tokens(attn_term)
             + out_bias[depth]
         )
         first_in = rows + branch
@@ -135,11 +228,9 @@
             jnp.dot(middle, lift_weight, preferred_element_type=jnp.float32) + up_bias[depth]
         )
         hidden = gelu_exact(hidden_pre).astype(jnp.bfloat16)
-        ffn_term = jnp.dot(hidden, drop_weight, preferred_element_type=jnp.float32)
+        ffn_term = dot_nt(hidden, drop_flat)
         second_in = first + (
-            lax.psum_scatter(
-                ffn_term.astype(jnp.bfloat16), "tensor", scatter_dimension=0, tiled=True
-            ).astype(jnp.float32)
+            scatter_tokens(ffn_term)
             + down_bias[depth]
         )
         kept.append(
@@ -162,8 +253,7 @@
     mixed = rows.astype(jnp.bfloat16)
     grad = out_grad.astype(jnp.float32)
     weight_parts = [None] * layers
-    split_parts = [None] * layers
-    shared_parts = [None] * layers
+    small_parts = [None] * layers
     for depth in reversed(range(layers)):
         (
             rows_in,
@@ -179,23 +269,20 @@
             hidden,
             second_in,
         ) = kept[depth]
-        joint_weight, merge_weight, lift_weight, drop_weight = fetch(depth)
-        joint_flat = joint_weight.reshape(width, -1)
+        unused, joint_flat, merge_flat, lift_weight, drop_flat = gathered[depth]
         unused, norm_pull = jax.vjp(norm_rows, second_in, norm_gain[depth, 1], norm_bias[depth, 1])
         grad_second, gain_two, shift_two = norm_pull(grad)
         grad_ffn = grad_second.astype(jnp.bfloat16)
         drop_bias_grad = jnp.sum(grad_ffn.astype(jnp.float32), axis=0)
         grad_ffn_full = lax.all_gather(grad_ffn, "tensor", axis=0, tiled=True)
         drop_grad = jnp.dot(grad_ffn_full.T, hidden, preferred_element_type=jnp.float32)
-        grad_hidden = jnp.dot(grad_ffn_full, drop_weight.T, preferred_element_type=jnp.float32)
+        grad_hidden = jnp.dot(grad_ffn_full, drop_flat, preferred_element_type=jnp.float32)
         unused, gelu_pull = jax.vjp(gelu_exact, hidden_pre)
         grad_pre = gelu_pull(grad_hidden)[0].astype(jnp.bfloat16)
         lift_bias_grad = jnp.sum(grad_pre.astype(jnp.float32), axis=0)
         lift_grad = jnp.dot(middle.T, grad_pre, preferred_element_type=jnp.float32)
         lift_term = jnp.dot(grad_pre, lift_weight.T, preferred_element_type=jnp.float32)
-        grad_first = grad_second + lax.psum_scatter(
-            lift_term.astype(jnp.bfloat16), "tensor", scatter_dimension=0, tiled=True
-        ).astype(jnp.float32)
+        grad_first = grad_second + scatter_tokens(lift_term)
         unused, norm_pull = jax.vjp(norm_rows, first_in, norm_gain[depth, 0], norm_bias[depth, 0])
         grad_first_in, gain_one, shift_one = norm_pull(grad_first)
         grad_branch = grad_first_in.astype(jnp.bfloat16)
@@ -203,7 +290,7 @@
         grad_branch_full = lax.all_gather(grad_branch, "tensor", axis=0, tiled=True)
         merge_grad = jnp.dot(grad_branch_full.T, heads_out, preferred_element_type=jnp.float32)
         grad_heads = jnp.dot(
-            grad_branch_full, merge_weight.T, preferred_element_type=jnp.float32
+            grad_branch_full, merge_flat, preferred_element_type=jnp.float32
         ).astype(jnp.bfloat16)
         grad_query, grad_keys, grad_values = lax.map(
             partial(attend_backward, scale=scale),
@@ -226,54 +313,41 @@
         ).astype(jnp.bfloat16)
         pair_bias_grad = jnp.sum(grad_joint[:, 0::2].astype(jnp.float32), axis=0)
         grad_flat = grad_joint.reshape(total_rows, -1)
-        joint_grad = jnp.dot(inputs.T, grad_flat, preferred_element_type=jnp.float32).reshape(
-            width, 3, -1
-        )
+        joint_grad = jnp.dot(inputs.T, grad_flat, preferred_element_type=jnp.float32)
         joint_term = jnp.dot(grad_flat, joint_flat.T, preferred_element_type=jnp.float32)
-        grad = grad_first_in + lax.psum_scatter(
-            joint_term.astype(jnp.bfloat16), "tensor", scatter_dimension=0, tiled=True
-        ).astype(jnp.float32)
+        grad = grad_first_in + scatter_tokens(joint_term)
         weight_parts[depth] = (
-            lax.psum_scatter(joint_grad, "dp", scatter_dimension=0, tiled=True),
-            lax.psum_scatter(merge_grad, "dp", scatter_dimension=0, tiled=True),
-            lax.psum_scatter(lift_grad, "dp", scatter_dimension=0, tiled=True),
-            lax.psum_scatter(drop_grad, "dp", scatter_dimension=0, tiled=True),
-        )
-        split_parts[depth] = (pair_bias_grad, lift_bias_grad)
-        shared_parts[depth] = (
-            merge_bias_grad,
-            jnp.stack([gain_one, gain_two]),
-            jnp.stack([shift_one, shift_two]),
-            drop_bias_grad,
-        )
-    stacks = [
+            scatter_rows(lift_grad[None], dp_size)[0],
+            scatter_rows(drop_grad[None], dp_size)[0],
+            scatter_rows(merge_grad[None], dp_size)[0],
+            scatter_rows(joint_grad[None], dp_size)[0],
+        )
+        small_parts[depth] = sum_small(
+            jnp.concatenate(
+                [merge_bias_grad, gain_one, gain_two, shift_one, shift_two, drop_bias_grad]
+            ),
+            jnp.concatenate([pair_bias_grad.reshape(-1), lift_bias_grad]),
+            dp_size,
+        )
+    lift_total, drop_total, merge_total, joint_total = [
         jnp.stack([weight_parts[depth][index] for depth in range(layers)]) for index in range(4)
     ]
-    merge_total = jnp.transpose(stacks[1], (0, 2, 1))
-    drop_total = jnp.transpose(stacks[3], (0, 2, 1))
-    pair_stack = jnp.stack([split_parts[depth][0] for depth in range(layers)])
-    lift_bias_stack = jnp.stack([split_parts[depth][1] for depth in range(layers)])
-    pair_total, lift_bias_total = lax.psum((pair_stack, lift_bias_stack), "dp")
-    merge_bias_stack = jnp.stack([shared_parts[depth][0] for depth in range(layers)])
-    gain_stack = jnp.stack([shared_parts[depth][1] for depth in range(layers)])
-    shift_stack = jnp.stack([shared_parts[depth][2] for depth in range(layers)])
-    drop_bias_stack = jnp.stack([shared_parts[depth][3] for depth in range(layers)])
-    merge_bias_total, gain_total, shift_total, drop_bias_total = lax.psum(
-        (merge_bias_stack, gain_stack, shift_stack, drop_bias_stack), ("dp", "tensor")
-    )
+    shared = jnp.stack([item[0] for item in small_parts]).reshape(layers, 6, width)
+    split = jnp.stack([item[1] for item in small_parts])
+    pair_size = 2 * qv_bias.shape[2]
     return (
         mixed,
         grad,
-        stacks[0],
-        pair_total,
-        merge_total,
-        merge_bias_total,
-        gain_total,
-        shift_total,
-        stacks[2],
-        lift_bias_total,
-        drop_total,
-        drop_bias_total,
+        joint_total.reshape(qkv_weight.shape),
+        split[:, :pair_size].reshape(qv_bias.shape),
+        jnp.transpose(merge_total, (0, 2, 1)),
+        shared[:, 0],
+        shared[:, 1:3],
+        shared[:, 3:5],
+        lift_total,
+        split[:, pair_size:],
+        jnp.transpose(drop_total, (0, 2, 1)),
+        shared[:, 5],
     )
 
 
@@ -308,5 +382,6 @@
         P(),
     )
     return jax.shard_map(
-        per_device, mesh=mesh, in_specs=in_specs, out_specs=out_specs, check_vma=False
-    )
+        partial(per_device, mesh.shape["dp"]),
+        mesh=mesh, in_specs=in_specs, out_specs=out_specs, check_vma=False
+    )

time: 1150 us -> 602 us (0.52)
  waiting for transfers between devices: 679 us -> 193 us
  blocking collectives: 282 us -> 66.6 us
  starting transfers between devices: 1.47 us -> 80.4 us
  local copies, waits for them, and re-layouts: 50.8 us -> 118 us
  between operations: 17.3 us -> 3.19 us
  other arithmetic: 37.4 us -> 49.3 us
    reduce_scatter x16 -> x0, waiting for transfers between devices: 585 us -> none  [the longest x2 142 us: per_device(): lax.psum_scatter(drop_grad, 'dp', scatter_dimension=0, tiled=True)]
    ppermute x0 -> x110, waiting for transfers between devices: none -> 193 us  [the longest x36 112 us: ring(): return lax.ppermute(block, 'dp', [(i, (i + 2) % 8) for i in range(8)])]
    all_gather x4 -> x0, blocking collectives: 138 us -> none  [the longest x2 73.8 us: fetch(): lax.all_gather(qkv_weight[depth], 'dp', axis=0, tiled=True)]
    all_gather x4 -> x0, waiting for transfers between devices: 92.5 us -> none  [the longest x2 72.3 us: fetch(): lax.all_gather(down_weight[depth], 'dp', axis=1, tiled=True)]
    ppermute x0 -> x110, starting transfers between devices: none -> 80.4 us  [the longest x74 66 us: swap(): return lax.ppermute(block, axis, [(i, i ^ bit) for i in range(size)])]
    psum x2 -> x0, blocking collectives: 75.1 us -> none  [the longest x1 38 us: per_device(): lax.psum((merge_bias_stack, gain_stack, shift_stack, drop_bias_stack), ('...]
    dynamic_update_slice x0 -> x30, local copies, waits for them, and re-layouts: none -> 25.8 us  [gather_rows(): lax.dynamic_update_slice(whole, block[:, None, None], (0, place, side, 0,...]
    unnamed x201 -> x257, local copies, waits for them, and re-layouts: 12.9 us -> 27.5 us
  transfers between devices with their start and end apart: 20 -> 110, of which waited for: 18 -> 46; matrix products, arithmetic and copies ran while one was open for 6% -> 24% of each run, Pallas kernels for 0% -> 0%
where the time goes in v1:
time: 602 us; the launch traced here: 591 us
  waiting for transfers between devices  193 us (32%)
  local copies, waits for them, and re-layouts  118 us (20%)
  starting transfers between devices  80.4 us (13%)
  matrix products  79.4 us (13%)
  blocking collectives  66.6 us (11%)
  other arithmetic  49.3 us (8%)
    ppermute x36, waiting for transfers between devices, ring(): return lax.ppermute(block, 'dp', [(i, (i + 2) % 8) for i in range(8)])  112 us
    ppermute x74, waiting for transfers between devices, swap(): return lax.ppermute(block, axis, [(i, i ^ bit) for i in range(size)])  81.5 us
    ppermute x74, starting transfers between devices, swap(): return lax.ppermute(block, axis, [(i, i ^ bit) for i in range(size)])  66 us
    unnamed x257, local copies, waits for them, and re-layouts  27.5 us
    dynamic_update_slice x30, local copies, waits for them, and re-layouts, gather_rows(): lax.dynamic_update_slice(whole, block[:, None, None], (0, place, side, 0,...  25.8 us
    all_gather x2, blocking collectives, per_device(): lax.all_gather(first.astype(jnp.bfloat16), 'tensor', axis=0, tiled=True)  17.1 us
    all_gather x2, blocking collectives, per_device(): grad_branch_full = lax.all_gather(grad_branch, 'tensor', axis=0, tiled=True)  16.8 us
    all_gather x2, blocking collectives, per_device(): lax.all_gather(rows.astype(jnp.bfloat16), 'tensor', axis=0, tiled=True)  16.6 us
  transfers between devices with their start and end apart: 110, of which 46 were waited for; matrix products, arithmetic and copies ran while one was open for 24% of the time, Pallas kernels for 0%

profile of v1, /device:TPU:0, one launch (start us, length us, event | category | flops | bytes accessed | tf_op | source)
XLA Modules:
  0.0 591.1 jit_solution(6240618630176297222)
XLA Ops:
  15.3 8.6 %all_gather.24 = bf16[512,768]{1,0:T(8,128)(2,1)S(1)} all-gather(bf16[128,768]{1,0:T(8,128)(2,1)S(1)} %copy-done.50), channel_id=1, replica_groups=mesh['dp'=8,'tensor'=4] {'tensor'}, dimensions={0}, use_global_device_ids=true | all-gather | bytes 983040 | tf_op jit(solution)/shard_map/all_gather | solution.py:205
  64.0 7.9 %collective-permute-done.4 = bf16[1,96,768]{1,2,0:T(8,128)(2,1)} collective-permute-done((bf16[1,96,768]{1,2,0:T(8,128)(2,1)}, bf16[1,96,768]{1,2,0:T(8,128)(2,1)}, u32[]{:S(2)}, u32[]{:S(2)}) %collective-permute-start.4) | collective-permute-done | bytes 147488 | tf_op jit(solution)/shard_map/ppermute | solution.py:71
  88.7 10.2 %while.52 = (s32[]{:T(128)}, bf16[3,512,64]{1,2,0:T(8,128)(2,1)}, f32[3,512]{1,0:T(4,128)S(1)}, s32[3,512]{1,0:T(4,128)S(1)}, bf16[3,512,64]{2,1,0:T(8,128)(2,1)...) while((s32[]{:T(128)}, bf16[3,512,64]{1,2,0:T(8,128)(2,1)}, ...), condition=%wide.region_3.4_spmd, body=%wide.region_0.3_spmd.sunk | while | flops 69209600 | bytes 3711077 | solution.py:215
  125.3 9.1 %collective-permute-done.33 = bf16[2,96,768]{2,1,0:T(8,128)(2,1)S(1)} collective-permute-done((bf16[2,96,768]{2,1,0:T(8,128)(2,1)S(1)}, bf16[2,96,768]{2,1,0:T(8,128)(2,1)S(1)}, u32[]{:S(2)}, u32[]{:S(2)}) %collective-permute-start.33) | collective-permute-done | bytes 294944 | tf_op jit(solution)/shard_map/ppermute | solution.py:71
  138.1 8.5 %all_gather.25 = bf16[512,768]{1,0:T(8,128)(2,1)S(1)} all-gather(bf16[128,768]{1,0:T(8,128)(2,1)S(1)} %fusion.140), channel_id=1, replica_groups=mesh['dp'=8,'tensor'=4] {'tensor'}, dimensions={0}, use_global_device_ids=true | all-gather | bytes 983040 | tf_op jit(solution)/shard_map/all_gather | solution.py:226
  163.1 7.9 %all_gather.26 = bf16[512,768]{1,0:T(8,128)(2,1)S(1)} all-gather(bf16[128,768]{1,0:T(8,128)(2,1)S(1)} %fusion.141), channel_id=1, replica_groups=mesh['dp'=8,'tensor'=4] {'tensor'}, dimensions={0}, use_global_device_ids=true | all-gather | bytes 983040 | tf_op jit(solution)/shard_map/all_gather | solution.py:205
  175.4 7.5 %while.53 = (s32[]{:T(128)}, bf16[3,512,64]{1,2,0:T(8,128)(2,1)}, f32[3,512]{1,0:T(4,128)S(1)}, s32[3,512]{1,0:T(4,128)S(1)}, bf16[3,512,64]{2,1,0:T(8,128)(2,1)...) while((s32[]{:T(128)}, bf16[3,512,64]{1,2,0:T(8,128)(2,1)}, ...), condition=%wide.region_11.12_spmd, body=%wide.region_8.11_spmd.sunk | while | flops 69209600 | bytes 3711077 | solution.py:215
  195.5 8.6 %all_gather.27 = bf16[512,768]{1,0:T(8,128)(2,1)S(1)} all-gather(bf16[128,768]{1,0:T(8,128)(2,1)S(1)} %fusion.142), channel_id=1, replica_groups=mesh['dp'=8,'tensor'=4] {'tensor'}, dimensions={0}, use_global_device_ids=true | all-gather | bytes 983040 | tf_op jit(solution)/shard_map/all_gather | solution.py:226
  224.6 7.9 %all_gather.28 = bf16[512,768]{1,0:T(8,128)(2,1)S(1)} all-gather(bf16[128,768]{1,0:T(8,128)(2,1)S(1)} %get-tuple-element.375), channel_id=1, replica_groups=mesh['dp'=8,'tensor'=4] {'tensor'}, dimensions={0}, use_global_device_ids=true | all-gather | bytes 983040 | tf_op jit(solution)/shard_map/all_gather | solution.py:277
  243.6 11.5 %collective-permute-done.89 = bf16[1,96,768]{2,1,0:T(8,128)(2,1)S(1)} collective-permute-done((bf16[1,96,768]{2,1,0:T(8,128)(2,1)S(1)}, bf16[1,96,768]{2,1,0:T(8,128)(2,1)S(1)}, u32[]{:S(2)}, u32[]{:S(2)}) %collective-permute-start.89) | collective-permute-done | bytes 147488 | tf_op jit(solution)/shard_map/ppermute | solution.py:71
  256.4 5.9 collective-permute-done.104
  263.4 5.8 collective-permute-done.90
  270.5 6.7 %collective-permute-done.106 = bf16[1,96,768]{2,1,0:T(8,128)(2,1)S(1)} collective-permute-done((bf16[1,96,768]{2,1,0:T(8,128)(2,1)S(1)}, bf16[1,96,768]{2,1,0:T(8,128)(2,1)S(1)}, u32[]{:S(2)}, u32[]{:S(2)}) %collective-permute-start.106) | collective-permute-done | bytes 147488 | tf_op jit(solution)/shard_map/ppermute | solution.py:75
  289.5 8.6 %all_gather.29 = bf16[512,768]{1,0:T(8,128)(2,1)S(1)} all-gather(bf16[128,768]{1,0:T(8,128)(2,1)S(1)} %get-tuple-element.377), channel_id=1, replica_groups=mesh['dp'=8,'tensor'=4] {'tensor'}, dimensions={0}, use_global_device_ids=true | all-gather | bytes 983040 | tf_op jit(solution)/shard_map/all_gather | solution.py:290
  302.7 25.0 %while.54 = (s32[]{:T(128)}, bf16[3,512,64]{1,2,0:T(8,128)(2,1)}, bf16[3,512,64]{1,2,0:T(8,128)(2,1)}, bf16[3,512,64]{1,2,0:T(8,128)(2,1)}, s32[3,512]{1,0:T(4,1...) while((s32[]{:T(128)}, bf16[3,512,64]{1,2,0:T(8,128)(2,1)}, ...), condition=%wide.region_22.23_spmd, body=%wide.region_20.22_spmd.sunk | while | flops 170458624 | bytes 12344549 | solution.py:295
  416.4 8.3 %all_gather.30 = bf16[512,768]{1,0:T(8,128)(2,1)S(1)} all-gather(bf16[128,768]{1,0:T(8,128)(2,1)S(1)} %get-tuple-element.369), channel_id=1, replica_groups=mesh['dp'=8,'tensor'=4] {'tensor'}, dimensions={0}, use_global_device_ids=true | all-gather | bytes 983040 | tf_op jit(solution)/shard_map/all_gather | solution.py:277
  434.9 9.5 %collective-permute-done.82 = bf16[1,96,768]{2,1,0:T(8,128)(2,1)S(1)} collective-permute-done((bf16[1,96,768]{2,1,0:T(8,128)(2,1)S(1)}, bf16[1,96,768]{2,1,0:T(8,128)(2,1)S(1)}, u32[]{:S(2)}, u32[]{:S(2)}) %collective-permute-start.82) | collective-permute-done | bytes 147488 | tf_op jit(solution)/shard_map/ppermute | solution.py:71
  445.5 6.0 %collective-permute-done.97 = bf16[1,96,768]{2,1,0:T(8,128)(2,1)S(1)} collective-permute-done((bf16[1,96,768]{2,1,0:T(8,128)(2,1)S(1)}, bf16[1,96,768]{2,1,0:T(8,128)(2,1)S(1)}, u32[]{:S(2)}, u32[]{:S(2)}) %collective-permute-start.97) | collective-permute-done | bytes 147488 | tf_op jit(solution)/shard_map/ppermute | solution.py:75
  459.8 6.7 %collective-permute-done.99 = bf16[1,96,768]{2,1,0:T(8,128)(2,1)S(1)} collective-permute-done((bf16[1,96,768]{2,1,0:T(8,128)(2,1)S(1)}, bf16[1,96,768]{2,1,0:T(8,128)(2,1)S(1)}, u32[]{:S(2)}, u32[]{:S(2)}) %collective-permute-start.99) | collective-permute-done | bytes 147488 | tf_op jit(solution)/shard_map/ppermute | solution.py:75
  468.4 6.2 %collective-permute-done.101 = bf16[1,96,768]{2,1,0:T(8,128)(2,1)S(1)} collective-permute-done((bf16[1,96,768]{2,1,0:T(8,128)(2,1)S(1)}, bf16[1,96,768]{2,1,0:T(8,128)(2,1)S(1)}, u32[]{:S(2)}, u32[]{:S(2)}) %collective-permute-start.101) | collective-permute-done | bytes 147488 | tf_op jit(solution)/shard_map/ppermute | solution.py:75
  479.8 8.2 %all_gather.31 = bf16[512,768]{1,0:T(8,128)(2,1)S(1)} all-gather(bf16[128,768]{1,0:T(8,128)(2,1)S(1)} %get-tuple-element.371), channel_id=1, replica_groups=mesh['dp'=8,'tensor'=4] {'tensor'}, dimensions={0}, use_global_device_ids=true | all-gather | bytes 983040 | tf_op jit(solution)/shard_map/all_gather | solution.py:290
  489.6 12.4 %while.55 = (s32[]{:T(128)}, bf16[3,512,64]{1,2,0:T(8,128)(2,1)S(1)}, bf16[3,512,64]{1,2,0:T(8,128)(2,1)S(1)}, bf16[3,512,64]{1,2,0:T(8,128)(2,1)}, s32[3,512]{1...) while((s32[]{:T(128)}, ...), condition=%wide.region_29.30_spmd, body=%wide.region_27.29_spmd.sunk | while | flops 170458624 | bytes 9198709 | solution.py:295
  565.5 5.8 collective-permute-done.45
  574.0 5.9 %collective-permute-done.47 = bf16[1,96,576]{2,1,0:T(8,128)(2,1)S(1)} collective-permute-done((bf16[1,96,576]{2,1,0:T(8,128)(2,1)S(1)}, bf16[1,96,576]{2,1,0:T(8,128)(2,1)S(1)}, u32[]{:S(2)}, u32[]{:S(2)}) %collective-permute-start.47) | collective-permute-done | bytes 110624 | tf_op jit(solution)/shard_map/ppermute | solution.py:75
  (847 shorter events, 433.9 us)
Async XLA Ops:
  3.5 41.2 %collective-permute-start.9 = (bf16[2,96,768]{2,1,0:T(8,128)(2,1)}, bf16[2,96,768]{2,1,0:T(8,128)(2,1)}, u32[]{:S(2)}, u32[]{:S(2)}) collective-permute-start(bf16[2,96,768]{2,1,0:T(8,128)(2,1)} %pad_maximum_fusion.2), channel_id=1, source_target_pairs={{0,4},{4,0},{8,12},{12,8},{16,20},{20,16},{24,28},{28,24},{1,5},{5... | collective-permute-start | bytes 884744 | tf_op jit(solution)/shard_map/ppermute | solution.py:71
  6.4 40.0 %collective-permute-start.10 = (bf16[2,96,768]{2,1,0:T(8,128)(2,1)}, bf16[2,96,768]{2,1,0:T(8,128)(2,1)}, u32[]{:S(2)}, u32[]{:S(2)}) collective-permute-start(bf16[2,96,768]{2,1,0:T(8,128)(2,1)} %pad_maximum_fusion.2), channel_id=1, source_target_pairs={{0,8},{4,12},{8,16},{12,20},{16,24},{20,28},{24,0},{28,4},{1,9},{5... | collective-permute-start | bytes 884744 | tf_op jit(solution)/shard_map/ppermute | solution.py:75
  9.0 28.5 %collective-permute-start = (bf16[1,96,768]{1,2,0:T(8,128)(2,1)}, bf16[1,96,768]{1,2,0:T(8,128)(2,1)}, u32[]{:S(2)}, u32[]{:S(2)}) collective-permute-start(bf16[1,96,768]{1,2,0:T(8,128)(2,1)} %get-tuple-element.460), channel_id=1, source_target_pairs={{0,4},{4,0},{8,12},{12,8},{16,20},{20,16},{24,28},{28,24},{1,5},{5... | collective-permute-start | bytes 442376 | tf_op jit(solution)/shard_map/ppermute | solution.py:71
  9.5 29.7 %collective-permute-start.1 = (bf16[1,96,768]{1,2,0:T(8,128)(2,1)}, bf16[1,96,768]{1,2,0:T(8,128)(2,1)}, u32[]{:S(2)}, u32[]{:S(2)}) collective-permute-start(bf16[1,96,768]{1,2,0:T(8,128)(2,1)} %get-tuple-element.460), channel_id=1, source_target_pairs={{0,8},{4,12},{8,16},{12,20},{16,24},{20,28},{24,0},{28,4},{1,9},{5... | collective-permute-start | bytes 442376 | tf_op jit(solution)/shard_map/ppermute | solution.py:75
  53.6 45.8 %collective-permute-start.11 = (bf16[2,96,768]{2,1,0:T(8,128)(2,1)}, bf16[2,96,768]{2,1,0:T(8,128)(2,1)}, u32[]{:S(2)}, u32[]{:S(2)}) collective-permute-start(bf16[2,96,768]{2,1,0:T(8,128)(2,1)} %collective-permute-done.10), channel_id=1, source_target_pairs={{0,4},{4,0},{8,12},{12,8},{16,20},{20,16},{24,28},{28,24},{1,5},{5... | collective-permute-start | bytes 884744 | tf_op jit(solution)/shard_map/ppermute | solution.py:71
  55.9 45.0 %collective-permute-start.12 = (bf16[2,96,768]{2,1,0:T(8,128)(2,1)}, bf16[2,96,768]{2,1,0:T(8,128)(2,1)}, u32[]{:S(2)}, u32[]{:S(2)}) collective-permute-start(bf16[2,96,768]{2,1,0:T(8,128)(2,1)} %collective-permute-done.10), channel_id=1, source_target_pairs={{0,8},{4,12},{8,16},{12,20},{16,24},{20,28},{24,0},{28,4},{1,9},{5... | collective-permute-start | bytes 884744 | tf_op jit(solution)/shard_map/ppermute | solution.py:75
  58.7 47.7 %collective-permute-start.29 = (bf16[2,96,768]{2,1,0:T(8,128)(2,1)}, bf16[2,96,768]{2,1,0:T(8,128)(2,1)}, u32[]{:S(2)}, u32[]{:S(2)}) collective-permute-start(bf16[2,96,768]{2,1,0:T(8,128)(2,1)} %collective-permute-done.28), channel_id=1, source_target_pairs={{0,4},{4,0},{8,12},{12,8},{16,20},{20,16},{24,28},{28,24},{1,5},{5... | collective-permute-start | bytes 884744 | tf_op jit(solution)/shard_map/ppermute | solution.py:71
  71.9 36.2 %collective-permute-start.30 = (bf16[2,96,768]{2,1,0:T(8,128)(2,1)}, bf16[2,96,768]{2,1,0:T(8,128)(2,1)}, u32[]{:S(2)}, u32[]{:S(2)}) collective-permute-start(bf16[2,96,768]{2,1,0:T(8,128)(2,1)} %collective-permute-done.28), channel_id=1, source_target_pairs={{0,8},{4,12},{8,16},{12,20},{16,24},{20,28},{24,0},{28,4},{1,9},{5... | collective-permute-start | bytes 884744 | tf_op jit(solution)/shard_map/ppermute | solution.py:75
  98.9 54.5 %collective-permute-start.22 = (bf16[1,96,768]{2,1,0:T(8,128)(2,1)}, bf16[1,96,768]{2,1,0:T(8,128)(2,1)}, u32[]{:S(2)}, u32[]{:S(2)}) collective-permute-start(bf16[1,96,768]{2,1,0:T(8,128)(2,1)} %collective-permute-done.21), channel_id=1, source_target_pairs={{0,4},{4,0},{8,12},{12,8},{16,20},{20,16},{24,28},{28,24},{1,5},{5... | collective-permute-start | bytes 442376 | tf_op jit(solution)/shard_map/ppermute | solution.py:71
  99.4 56.9 %collective-permute-start.24 = (bf16[1,96,768]{2,1,0:T(8,128)(2,1)}, bf16[1,96,768]{2,1,0:T(8,128)(2,1)}, u32[]{:S(2)}, u32[]{:S(2)}) collective-permute-start(bf16[1,96,768]{2,1,0:T(8,128)(2,1)} %collective-permute-done.23), channel_id=1, source_target_pairs={{0,4},{4,0},{8,12},{12,8},{16,20},{20,16},{24,28},{28,24},{1,5},{5... | collective-permute-start | bytes 442376 | tf_op jit(solution)/shard_map/ppermute | solution.py:71
  239.2 31.0 %collective-permute-start.36 = (bf16[2,128,768]{2,1,0:T(8,128)(2,1)S(1)}, bf16[2,128,768]{2,1,0:T(8,128)(2,1)S(1)}, u32[]{:S(2)}, u32[]{:S(2)}) collective-permute-start(bf16[2,128,768]{2,1,0:T(8,128)(2,1)S(1)} %fusion.116), channel_id=1, source_target_pairs={{0,1},{1,0},{2,3},{3,2},{4,5},{5,4},{6,7},{7,6},{8,9},{9,8},{10,11... | collective-permute-start | bytes 1179656 | tf_op jit(solution)/shard_map/ppermute | solution.py:71
  240.9 29.6 %collective-permute-start.107 = (bf16[1,96,768]{2,1,0:T(8,128)(2,1)S(1)}, bf16[1,96,768]{2,1,0:T(8,128)(2,1)S(1)}, u32[]{:S(2)}, u32[]{:S(2)}) collective-permute-start(bf16[1,96,768]{2,1,0:T(8,128)(2,1)S(1)} %get-tuple-element.419), channel_id=1, source_target_pairs={{0,4},{4,0},{8,12},{12,8},{16,20},{20,16},{24,28},{28,24},{1,5},{5... | collective-permute-start | bytes 442376 | tf_op jit(solution)/shard_map/ppermute | solution.py:71
  241.4 38.2 %collective-permute-start.109 = (bf16[1,96,768]{2,1,0:T(8,128)(2,1)S(1)}, bf16[1,96,768]{2,1,0:T(8,128)(2,1)S(1)}, u32[]{:S(2)}, u32[]{:S(2)}) collective-permute-start(bf16[1,96,768]{2,1,0:T(8,128)(2,1)S(1)} %get-tuple-element.418), channel_id=1, source_target_pairs={{0,4},{4,0},{8,12},{12,8},{16,20},{20,16},{24,28},{28,24},{1,5},{5... | collective-permute-start | bytes 442376 | tf_op jit(solution)/shard_map/ppermute | solution.py:71
  337.4 69.4 %collective-permute-start.38 = (bf16[2,128,768]{2,1,0:T(8,128)(2,1)}, bf16[2,128,768]{2,1,0:T(8,128)(2,1)}, u32[]{:S(2)}, u32[]{:S(2)}) collective-permute-start(bf16[2,128,768]{2,1,0:T(8,128)(2,1)} %fusion.117), channel_id=1, source_target_pairs={{0,1},{1,0},{2,3},{3,2},{4,5},{5,4},{6,7},{7,6},{8,9},{9,8},{10,11... | collective-permute-start | bytes 1179656 | tf_op jit(solution)/shard_map/ppermute | solution.py:71
  355.9 29.3 %collective-permute-start.75 = (bf16[1,96,192]{2,1,0:T(8,128)(2,1)}, bf16[1,96,192]{2,1,0:T(8,128)(2,1)}, u32[]{:S(2)}, u32[]{:S(2)}) collective-permute-start(bf16[1,96,192]{2,1,0:T(8,128)(2,1)} %get-tuple-element.451), channel_id=1, source_target_pairs={{0,4},{4,0},{8,12},{12,8},{16,20},{20,16},{24,28},{28,24},{1,5},{5... | collective-permute-start | bytes 110600 | tf_op jit(solution)/shard_map/ppermute | solution.py:71
  363.6 34.7 %collective-permute-start.77 = (bf16[1,96,192]{2,1,0:T(8,128)(2,1)}, bf16[1,96,192]{2,1,0:T(8,128)(2,1)}, u32[]{:S(2)}, u32[]{:S(2)}) collective-permute-start(bf16[1,96,192]{2,1,0:T(8,128)(2,1)} %get-tuple-element.450), channel_id=1, source_target_pairs={{0,4},{4,0},{8,12},{12,8},{16,20},{20,16},{24,28},{28,24},{1,5},{5... | collective-permute-start | bytes 110600 | tf_op jit(solution)/shard_map/ppermute | solution.py:71
  427.7 32.0 %collective-permute-start.100 = (bf16[1,96,768]{2,1,0:T(8,128)(2,1)S(1)}, bf16[1,96,768]{2,1,0:T(8,128)(2,1)S(1)}, u32[]{:S(2)}, u32[]{:S(2)}) collective-permute-start(bf16[1,96,768]{2,1,0:T(8,128)(2,1)S(1)} %get-tuple-element.415), channel_id=1, source_target_pairs={{0,4},{4,0},{8,12},{12,8},{16,20},{20,16},{24,28},{28,24},{1,5},{5... | collective-permute-start | bytes 442376 | tf_op jit(solution)/shard_map/ppermute | solution.py:71
  428.7 39.7 %collective-permute-start.102 = (bf16[1,96,768]{2,1,0:T(8,128)(2,1)S(1)}, bf16[1,96,768]{2,1,0:T(8,128)(2,1)S(1)}, u32[]{:S(2)}, u32[]{:S(2)}) collective-permute-start(bf16[1,96,768]{2,1,0:T(8,128)(2,1)S(1)} %get-tuple-element.414), channel_id=1, source_target_pairs={{0,4},{4,0},{8,12},{12,8},{16,20},{20,16},{24,28},{28,24},{1,5},{5... | collective-permute-start | bytes 442376 | tf_op jit(solution)/shard_map/ppermute | solution.py:71
  433.6 25.9 %collective-permute-start.40 = (bf16[2,128,768]{2,1,0:T(8,128)(2,1)S(1)}, bf16[2,128,768]{2,1,0:T(8,128)(2,1)S(1)}, u32[]{:S(2)}, u32[]{:S(2)}) collective-permute-start(bf16[2,128,768]{2,1,0:T(8,128)(2,1)S(1)} %fusion.118), channel_id=1, source_target_pairs={{0,1},{1,0},{2,3},{3,2},{4,5},{5,4},{6,7},{7,6},{8,9},{9,8},{10,11... | collective-permute-start | bytes 1179656 | tf_op jit(solution)/shard_map/ppermute | solution.py:71
  521.2 31.7 %collective-permute-start.68 = (bf16[1,96,192]{2,1,0:T(8,128)(2,1)}, bf16[1,96,192]{2,1,0:T(8,128)(2,1)}, u32[]{:S(2)}, u32[]{:S(2)}) collective-permute-start(bf16[1,96,192]{2,1,0:T(8,128)(2,1)} %get-tuple-element.447), channel_id=1, source_target_pairs={{0,4},{4,0},{8,12},{12,8},{16,20},{20,16},{24,28},{28,24},{1,5},{5... | collective-permute-start | bytes 110600 | tf_op jit(solution)/shard_map/ppermute | solution.py:71
  522.2 36.6 %collective-permute-start.70 = (bf16[1,96,192]{2,1,0:T(8,128)(2,1)}, bf16[1,96,192]{2,1,0:T(8,128)(2,1)}, u32[]{:S(2)}, u32[]{:S(2)}) collective-permute-start(bf16[1,96,192]{2,1,0:T(8,128)(2,1)} %get-tuple-element.446), channel_id=1, source_target_pairs={{0,4},{4,0},{8,12},{12,8},{16,20},{20,16},{24,28},{28,24},{1,5},{5... | collective-permute-start | bytes 110600 | tf_op jit(solution)/shard_map/ppermute | solution.py:71
  533.2 25.4 %collective-permute-start.44 = (bf16[1,96,576]{2,1,0:T(8,128)(2,1)S(1)}, bf16[1,96,576]{2,1,0:T(8,128)(2,1)S(1)}, u32[]{:S(2)}, u32[]{:S(2)}) collective-permute-start(bf16[1,96,576]{2,1,0:T(8,128)(2,1)S(1)} %get-tuple-element.433), channel_id=1, source_target_pairs={{0,4},{4,0},{8,12},{12,8},{16,20},{20,16},{24,28},{28,24},{1,5},{5... | collective-permute-start | bytes 331784 | tf_op jit(solution)/shard_map/ppermute | solution.py:71
  541.3 24.2 %collective-permute-start.46 = (bf16[1,96,576]{2,1,0:T(8,128)(2,1)}, bf16[1,96,576]{2,1,0:T(8,128)(2,1)}, u32[]{:S(2)}, u32[]{:S(2)}) collective-permute-start(bf16[1,96,576]{2,1,0:T(8,128)(2,1)} %get-tuple-element.436), channel_id=1, source_target_pairs={{0,4},{4,0},{8,12},{12,8},{16,20},{20,16},{24,28},{28,24},{1,5},{5... | collective-permute-start | bytes 331784 | tf_op jit(solution)/shard_map/ppermute | solution.py:71
  556.8 26.6 %collective-permute-start.50 = (bf16[1,96,576]{2,1,0:T(8,128)(2,1)}, bf16[1,96,576]{2,1,0:T(8,128)(2,1)}, u32[]{:S(2)}, u32[]{:S(2)}) collective-permute-start(bf16[1,96,576]{2,1,0:T(8,128)(2,1)} %get-tuple-element.434), channel_id=1, source_target_pairs={{0,4},{4,0},{8,12},{12,8},{16,20},{20,16},{24,28},{28,24},{1,5},{5... | collective-permute-start | bytes 331784 | tf_op jit(solution)/shard_map/ppermute | solution.py:71
  (215 other events, 1887.5 us)

commit v2 on v1

--- a/solution.py
+++ b/solution.py
@@ -95,26 +95,60 @@
     return whole.reshape(pieces, 8 * count, cols)
 
 
-def scatter_rows(total, dp_size):
+def after(block, token):
+    mark = token[(0,) * token.ndim]
+    return block + jnp.where(mark != mark, 1.0, 0.0).astype(block.dtype)
+
+
+def scatter_steps(total, dp_size):
     if dp_size != 8:
-        return lax.psum_scatter(total, "dp", scatter_dimension=1, tiled=True)
+        yield lax.psum_scatter(total, "dp", scatter_dimension=1, tiled=True)
+        return
     pieces, rows, cols = total.shape
     me = lax.axis_index("dp")
     far, near = me // 2, me % 2
     parts = total.reshape(pieces, 4, 2, rows // 8, cols)
     away = lax.dynamic_index_in_dim(parts, 1 - near, 2, keepdims=False)
     home = lax.dynamic_index_in_dim(parts, near, 2, keepdims=False)
-    here = []
-    for step in range(4):
+    came = swap(away.astype(jnp.bfloat16), "dp", 1, 8)
+    token = yield None
+    if token is not None:
+        came = after(came, token)
+    pair = home.astype(jnp.float32) + came.astype(jnp.float32)
+    summed = lax.dynamic_index_in_dim(pair, (far - 1) % 4, 1, keepdims=False)
+    for step in range(1, 4):
+        came = ring(summed.astype(jnp.bfloat16))
+        token = yield None
+        if token is not None:
+            came = after(came, token)
         place = (far - 1 - step) % 4
-        sent = lax.dynamic_index_in_dim(away, place, 1, keepdims=False)
-        kept = lax.dynamic_index_in_dim(home, place, 1, keepdims=False)
-        came = swap(sent.astype(jnp.bfloat16), "dp", 1, 8)
-        here.append(kept.astype(jnp.float32) + came.astype(jnp.float32))
-    summed = here[0]
-    for step in range(1, 4):
-        summed = ring(summed.astype(jnp.bfloat16)).astype(jnp.float32) + here[step]
-    return summed
+        kept = lax.dynamic_index_in_dim(pair, place, 1, keepdims=False)
+        summed = came.astype(jnp.float32) + kept
+    yield summed
+
+
+class Sums:
+    def __init__(self, dp_size):
+        self.dp_size, self.open, self.done = dp_size, [], {}
+
+    def start(self, name, total):
+        self.open.append((name, scatter_steps(total, self.dp_size)))
+        self.take(self.open[-1], None, True)
+
+    def take(self, item, token, first=False):
+        name, steps = item
+        result = next(steps) if first else steps.send(token)
+        if result is not None:
+            self.done[name] = result
+            self.open.remove(item)
+
+    def move(self, token):
+        for item in list(self.open):
+            self.take(item, token)
+
+    def finish(self):
+        while self.open:
+            self.move(None)
 
 
 def scatter_tokens(term):
@@ -194,9 +228,8 @@
     for depth in range(layers):
         joint_shard, lift_shard = shards[depth]
         if depth > 0:
-            joint_shard, lift_shard, unused = lax.optimization_barrier(
-                (joint_shard, lift_shard, gathered[depth - 1][0])
-            )
+            joint_shard = after(joint_shard, gathered[depth - 1][0])
+            lift_shard = after(lift_shard, gathered[depth - 1][0])
         joint_all = gather_rows(joint_shard, dp_size)[0]
         lift_all = gather_rows(lift_shard, dp_size)
         joint_flat, merge_flat = joint_all[:, :joint_cols], joint_all[:, joint_cols:]
@@ -212,8 +245,8 @@
         query_blocks = to_blocks(query, seq_count, head_count)
         key_blocks = to_blocks(keys, seq_count, head_count)
         value_blocks = to_blocks(values, seq_count, head_count)
-        attended, totals = lax.map(
-            partial(attend_forward, scale=scale), (query_blocks, key_blocks, value_blocks, marks)
+        attended, totals = jax.vmap(partial(attend_forward, scale=scale))(
+            (query_blocks, key_blocks, value_blocks, marks)
         )
         heads_out = from_blocks(attended, seq_count, head_count).astype(jnp.bfloat16)
         attn_term = dot_nt(heads_out, merge_flat)
@@ -252,7 +285,7 @@
         rows = norm_rows(second_in, norm_gain[depth, 1], norm_bias[depth, 1])
     mixed = rows.astype(jnp.bfloat16)
     grad = out_grad.astype(jnp.float32)
-    weight_parts = [None] * layers
+    sums = Sums(dp_size)
     small_parts = [None] * layers
     for depth in reversed(range(layers)):
         (
@@ -279,21 +312,23 @@
         grad_hidden = jnp.dot(grad_ffn_full, drop_flat, preferred_element_type=jnp.float32)
         unused, gelu_pull = jax.vjp(gelu_exact, hidden_pre)
         grad_pre = gelu_pull(grad_hidden)[0].astype(jnp.bfloat16)
+        sums.move(grad_pre)
         lift_bias_grad = jnp.sum(grad_pre.astype(jnp.float32), axis=0)
         lift_grad = jnp.dot(middle.T, grad_pre, preferred_element_type=jnp.float32)
         lift_term = jnp.dot(grad_pre, lift_weight.T, preferred_element_type=jnp.float32)
+        sums.start(("lift", depth), jnp.stack([lift_grad, drop_grad]))
         grad_first = grad_second + scatter_tokens(lift_term)
         unused, norm_pull = jax.vjp(norm_rows, first_in, norm_gain[depth, 0], norm_bias[depth, 0])
         grad_first_in, gain_one, shift_one = norm_pull(grad_first)
         grad_branch = grad_first_in.astype(jnp.bfloat16)
         merge_bias_grad = jnp.sum(grad_branch.astype(jnp.float32), axis=0)
         grad_branch_full = lax.all_gather(grad_branch, "tensor", axis=0, tiled=True)
+        sums.move(grad_branch_full)
         merge_grad = jnp.dot(grad_branch_full.T, heads_out, preferred_element_type=jnp.float32)
         grad_heads = jnp.dot(
             grad_branch_full, merge_flat, preferred_element_type=jnp.float32
         ).astype(jnp.bfloat16)
-        grad_query, grad_keys, grad_values = lax.map(
-            partial(attend_backward, scale=scale),
+        grad_query, grad_keys, grad_values = jax.vmap(partial(attend_backward, scale=scale))(
             (
                 query_blocks,
                 key_blocks,
@@ -303,6 +338,7 @@
                 to_blocks(grad_heads, seq_count, head_count),
             ),
         )
+        sums.move(grad_values)
         grad_joint = jnp.stack(
             [
                 from_blocks(grad_query, seq_count, head_count),
@@ -314,26 +350,32 @@
         pair_bias_grad = jnp.sum(grad_joint[:, 0::2].astype(jnp.float32), axis=0)
         grad_flat = grad_joint.reshape(total_rows, -1)
         joint_grad = jnp.dot(inputs.T, grad_flat, preferred_element_type=jnp.float32)
+        sums.start(("joint", depth), jnp.concatenate([joint_grad, merge_grad], axis=1)[None])
         joint_term = jnp.dot(grad_flat, joint_flat.T, preferred_element_type=jnp.float32)
         grad = grad_first_in + scatter_tokens(joint_term)
-        weight_parts[depth] = (
-            scatter_rows(lift_grad[None], dp_size)[0],
-            scatter_rows(drop_grad[None], dp_size)[0],
-            scatter_rows(merge_grad[None], dp_size)[0],
-            scatter_rows(joint_grad[None], dp_size)[0],
-        )
-        small_parts[depth] = sum_small(
+        sums.move(grad if depth > 0 else None)
+        small_parts[depth] = (
             jnp.concatenate(
                 [merge_bias_grad, gain_one, gain_two, shift_one, shift_two, drop_bias_grad]
             ),
             jnp.concatenate([pair_bias_grad.reshape(-1), lift_bias_grad]),
-            dp_size,
-        )
-    lift_total, drop_total, merge_total, joint_total = [
-        jnp.stack([weight_parts[depth][index] for depth in range(layers)]) for index in range(4)
-    ]
-    shared = jnp.stack([item[0] for item in small_parts]).reshape(layers, 6, width)
-    split = jnp.stack([item[1] for item in small_parts])
+        )
+    shared, split = sum_small(
+        jnp.concatenate([item[0] for item in small_parts]),
+        jnp.concatenate([item[1] for item in small_parts]),
+        dp_size,
+    )
+    sums.finish()
+    joint_total = jnp.stack(
+        [sums.done["joint", depth][0][:, :joint_cols] for depth in range(layers)]
+    )
+    merge_total = jnp.stack(
+        [sums.done["joint", depth][0][:, joint_cols:] for depth in range(layers)]
+    )
+    lift_total = jnp.stack([sums.done["lift", depth][0] for depth in range(layers)])
+    drop_total = jnp.stack([sums.done["lift", depth][1] for depth in range(layers)])
+    shared = shared.reshape(layers, 6, width)
+    split = split.reshape(layers, -1)
     pair_size = 2 * qv_bias.shape[2]
     return (
         mixed,

time: 602 us -> 438 us (0.73)
  waiting for transfers between devices: 193 us -> 104 us
  matrix products: 79.4 us -> 51.9 us
  local copies, waits for them, and re-layouts: 118 us -> 92.8 us
  starting transfers between devices: 80.4 us -> 58.7 us
  between operations: 3.19 us -> 12.9 us
  other arithmetic: 49.3 us -> 42.5 us
    ppermute x36 -> x24, waiting for transfers between devices: 112 us -> 67.2 us  [ring(): return lax.ppermute(block, 'dp', [(i, (i + 2) % 8) for i in range(8)])]
    ppermute x74 -> x41, waiting for transfers between devices: 81.5 us -> 37 us  [swap(): return lax.ppermute(block, axis, [(i, i ^ bit) for i in range(size)])]
    ppermute x74 -> x41, starting transfers between devices: 66 us -> 43.8 us  [swap(): return lax.ppermute(block, axis, [(i, i ^ bit) for i in range(size)])]
    dynamic_update_slice x30 -> x29, local copies, waits for them, and re-layouts: 25.8 us -> 13.9 us  [gather_rows(): lax.dynamic_update_slice(whole, block[:, None, None], (0, place, side, 0,...]
    dot_general x12 -> x2, matrix products: 13.4 us -> 1.79 us  [block_scores(): scores = jnp.dot(query, keys.T, preferred_element_type=jnp.float32) * scale]
    while x30 -> x0, local copies, waits for them, and re-layouts: 9.74 us -> none  [the longest x6 5.75 us: per_device(): lax.map(partial(attend_forward, scale=scale), (query_blocks, key_blocks,...]
    concatenate x0 -> x4, local copies, waits for them, and re-layouts: none -> 8.46 us  [the longest x2 5.11 us: per_device(): jnp.concatenate([joint_grad, merge_grad], axis=1)[None]]
    another operation x18 -> x8, local copies, waits for them, and re-layouts: 9.41 us -> 1.45 us  [the longest x2 0.81 us: per_device(): jnp.stack([sums.done['joint', depth][0][:, joint_cols:] for depth in rang...]
  transfers between devices with their start and end apart: 110 -> 65, of which waited for: 46 -> 25; matrix products, arithmetic and copies ran while one was open for 24% -> 33% of each run, Pallas kernels for 0% -> 0%
where the time goes in v2:
time: 438 us; the launch traced here: 430 us
  waiting for transfers between devices  104 us (24%)
  local copies, waits for them, and re-layouts  92.8 us (21%)
  blocking collectives  66.6 us (15%)
  starting transfers between devices  58.7 us (13%)
  matrix products  51.9 us (12%)
  other arithmetic  42.5 us (10%)
  between operations  12.9 us (3%)
    ppermute x24, waiting for transfers between devices, ring(): return lax.ppermute(block, 'dp', [(i, (i + 2) % 8) for i in range(8)])  67.2 us
    ppermute x41, starting transfers between devices, swap(): return lax.ppermute(block, axis, [(i, i ^ bit) for i in range(size)])  43.8 us
    ppermute x41, waiting for transfers between devices, swap(): return lax.ppermute(block, axis, [(i, i ^ bit) for i in range(size)])  37 us
    unnamed x352, local copies, waits for them, and re-layouts  22 us
    all_gather x2, blocking collectives, per_device(): lax.all_gather(rows.astype(jnp.bfloat16), 'tensor', axis=0, tiled=True)  17.7 us
    all_gather x2, blocking collectives, per_device(): grad_ffn_full = lax.all_gather(grad_ffn, 'tensor', axis=0, tiled=True)  16.9 us
    all_gather x2, blocking collectives, per_device(): grad_branch_full = lax.all_gather(grad_branch, 'tensor', axis=0, tiled=True)  16.2 us
    all_gather x2, blocking collectives, per_device(): lax.all_gather(first.astype(jnp.bfloat16), 'tensor', axis=0, tiled=True)  15.9 us
  transfers between devices with their start and end apart: 65, of which 25 were waited for; matrix products, arithmetic and copies ran while one was open for 33% of the time, Pallas kernels for 0%

profile of v2, /device:TPU:0, one launch (start us, length us, event | category | flops | bytes accessed | tf_op | source)
XLA Modules:
  0.0 429.8 jit_solution(17220050295716035370)
XLA Ops:
  15.8 9.1 %all_gather.24 = bf16[512,768]{1,0:T(8,128)(2,1)} all-gather(bf16[128,768]{1,0:T(8,128)(2,1)S(1)} %copy-done.73), channel_id=1, replica_groups=mesh['dp'=8,'tensor'=4] {'tensor'}, dimensions={0}, use_global_device_ids=true | all-gather | bytes 983040 | tf_op jit(solution)/shard_map/all_gather | solution.py:238
  59.6 3.4 collective-permute-done.4
  85.7 7.8 %collective-permute-done.14 = bf16[2,96,768]{2,1,0:T(8,128)(2,1)S(1)} collective-permute-done((bf16[2,96,768]{2,1,0:T(8,128)(2,1)}, bf16[2,96,768]{2,1,0:T(8,128)(2,1)S(1)}, u32[]{:S(2)}, u32[]{:S(2)}) %collective-permute-start.14) | collective-permute-done | bytes 294944 | tf_op jit(solution)/shard_map/ppermute | solution.py:75
  95.8 5.9 %collective-permute-done.15 = bf16[2,96,768]{2,1,0:T(8,128)(2,1)S(1)} collective-permute-done((bf16[2,96,768]{2,1,0:T(8,128)(2,1)S(1)}, bf16[2,96,768]{2,1,0:T(8,128)(2,1)S(1)}, u32[]{:S(2)}, u32[]{:S(2)}) %collective-permute-start.15) | collective-permute-done | bytes 294944 | tf_op jit(solution)/shard_map/ppermute | solution.py:71
  107.0 8.1 %all_gather.25 = bf16[512,768]{1,0:T(8,128)(2,1)S(1)} all-gather(bf16[128,768]{1,0:T(8,128)(2,1)S(1)} %fusion.78), channel_id=1, replica_groups=mesh['dp'=8,'tensor'=4] {'tensor'}, dimensions={0}, use_global_device_ids=true | all-gather | bytes 983040 | tf_op jit(solution)/shard_map/all_gather | solution.py:259
  115.1 5.5 %multiply_convert_fusion.3 = (bf16[512,768]{1,0:T(8,128)(2,1)S(1)}, f32[512,768]{1,0:T(8,128)}, f32[512,768]{1,0:T(8,128)}) fusion(f32[768]{0:T(1024)S(1)} %copy-done.146, bf16[512,768]{1,0:T(8,128)(2,1)S(1)} %all_gather.25, bf16[768,768]{1,0:T(8,128)(2,1)S(1)} %bitcast.614), kind=kOutput, calls=%fused_computation.53 | convolution fusion | flops 629932032 | bytes 5901312 | tf_op jit(solution)/shard_map/dot_general | solution.py:261
  125.8 7.1 %collective-permute-done.21 = bf16[1,96,768]{2,1,0:T(8,128)(2,1)S(1)} collective-permute-done((bf16[1,96,768]{2,1,0:T(8,128)(2,1)S(1)}, bf16[1,96,768]{2,1,0:T(8,128)(2,1)S(1)}, u32[]{:S(2)}, u32[]{:S(2)}) %collective-permute-start.21) | collective-permute-done | bytes 147488 | tf_op jit(solution)/shard_map/ppermute | solution.py:75
  146.0 8.6 %all_gather.26 = bf16[512,768]{1,0:T(8,128)(2,1)S(1)} all-gather(bf16[128,768]{1,0:T(8,128)(2,1)S(1)} %fusion.79), channel_id=1, replica_groups=mesh['dp'=8,'tensor'=4] {'tensor'}, dimensions={0}, use_global_device_ids=true | all-gather | bytes 983040 | tf_op jit(solution)/shard_map/all_gather | solution.py:238
  166.8 8.5 %collective-permute-done.32 = bf16[2,96,768]{2,1,0:T(8,128)(2,1)S(1)} collective-permute-done((bf16[2,96,768]{2,1,0:T(8,128)(2,1)}, bf16[2,96,768]{2,1,0:T(8,128)(2,1)S(1)}, u32[]{:S(2)}, u32[]{:S(2)}) %collective-permute-start.32) | collective-permute-done | bytes 294944 | tf_op jit(solution)/shard_map/ppermute | solution.py:75
  177.6 5.7 %collective-permute-done.33 = bf16[2,96,768]{2,1,0:T(8,128)(2,1)S(1)} collective-permute-done((bf16[2,96,768]{2,1,0:T(8,128)(2,1)S(1)}, bf16[2,96,768]{2,1,0:T(8,128)(2,1)S(1)}, u32[]{:S(2)}, u32[]{:S(2)}) %collective-permute-start.33) | collective-permute-done | bytes 294944 | tf_op jit(solution)/shard_map/ppermute | solution.py:71
  185.4 7.8 %all_gather.27 = bf16[512,768]{1,0:T(8,128)(2,1)S(1)} all-gather(bf16[128,768]{1,0:T(8,128)(2,1)S(1)} %fusion.80), channel_id=1, replica_groups=mesh['dp'=8,'tensor'=4] {'tensor'}, dimensions={0}, use_global_device_ids=true | all-gather | bytes 983040 | tf_op jit(solution)/shard_map/all_gather | solution.py:259
  193.2 10.2 %multiply_convert_fusion.2 = (bf16[512,768]{1,0:T(8,128)(2,1)S(1)}, f32[512,768]{1,0:T(8,128)S(1)}, f32[512,768]{1,0:T(8,128)S(1)}) fusion(f32[768]{0:T(1024)S(1)} %copy-done.145, bf16[512,768]{1,0:T(8,128)(2,1)S(1)} %all_gather.27, bf16[768,768]{1,0:T(8,128)(2,1)S(1)} %bitcast.618), kind=kOutput, calls=%fused_computation.40 | convolution fusion | flops 629932032 | bytes 5901312 | tf_op jit(solution)/shard_map/dot_general | solution.py:261
  208.0 5.6 %collective-permute-done.35 = bf16[128,768]{1,0:T(8,128)(2,1)S(1)} collective-permute-done((bf16[128,768]{1,0:T(8,128)(2,1)S(1)}, bf16[128,768]{1,0:T(8,128)(2,1)S(1)}, u32[]{:S(2)}, u32[]{:S(2)}) %collective-permute-start.35) | collective-permute-done | bytes 196640 | tf_op jit(solution)/shard_map/ppermute | solution.py:71
  216.5 8.6 %all_gather.28 = bf16[512,768]{1,0:T(8,128)(2,1)S(1)} all-gather(bf16[128,768]{1,0:T(8,128)(2,1)S(1)} %get-tuple-element.83), channel_id=1, replica_groups=mesh['dp'=8,'tensor'=4] {'tensor'}, dimensions={0}, use_global_device_ids=true | all-gather | bytes 983040 | tf_op jit(solution)/shard_map/all_gather | solution.py:310
  243.1 8.2 %all_gather.29 = bf16[512,768]{1,0:T(8,128)(2,1)S(1)} all-gather(bf16[128,768]{1,0:T(8,128)(2,1)S(1)} %get-tuple-element.85), channel_id=1, replica_groups=mesh['dp'=8,'tensor'=4] {'tensor'}, dimensions={0}, use_global_device_ids=true | all-gather | bytes 983040 | tf_op jit(solution)/shard_map/all_gather | solution.py:325
  284.4 3.4 collective-permute-done.39
  291.0 8.3 %all_gather.30 = bf16[512,768]{1,0:T(8,128)(2,1)S(1)} all-gather(bf16[128,768]{1,0:T(8,128)(2,1)S(1)} %get-tuple-element.87), channel_id=1, replica_groups=mesh['dp'=8,'tensor'=4] {'tensor'}, dimensions={0}, use_global_device_ids=true | all-gather | bytes 983040 | tf_op jit(solution)/shard_map/all_gather | solution.py:310
  314.2 12.7 %collective-permute-done.63 = bf16[2,96,768]{2,1,0:T(8,128)(2,1)S(1)} collective-permute-done((bf16[2,96,768]{2,1,0:T(8,128)(2,1)S(1)}, bf16[2,96,768]{2,1,0:T(8,128)(2,1)S(1)}, u32[]{:S(2)}, u32[]{:S(2)}) %collective-permute-start.63) | collective-permute-done | bytes 294944 | tf_op jit(solution)/shard_map/ppermute | solution.py:75
  329.6 7.9 %all_gather.31 = bf16[512,768]{1,0:T(8,128)(2,1)S(1)} all-gather(bf16[128,768]{1,0:T(8,128)(2,1)S(1)} %get-tuple-element.89), channel_id=1, replica_groups=mesh['dp'=8,'tensor'=4] {'tensor'}, dimensions={0}, use_global_device_ids=true | all-gather | bytes 983040 | tf_op jit(solution)/shard_map/all_gather | solution.py:325
  363.1 4.9 %collective-permute-start.54 = (f32[90,128]{1,0:T(8,128)S(1)}, f32[90,128]{1,0:T(8,128)S(1)}, u32[]{:S(2)}, u32[]{:S(2)}) collective-permute-start(f32[90,128]{1,0:T(8,128)S(1)} %fusion.211), channel_id=1, source_target_pairs={{0,16},{4,20},{8,24},{12,28},{16,0},{20,4},{24,8},{28,12},{1,17},{... | collective-permute-start | bytes 138248 | tf_op jit(solution)/shard_map/ppermute | solution.py:71
  390.1 3.9 collective-permute-done.45
  395.0 7.5 %collective-permute-done.46 = bf16[1,96,768]{2,1,0:T(8,128)(2,1)S(1)} collective-permute-done((bf16[1,96,768]{2,1,0:T(8,128)(2,1)S(1)}, bf16[1,96,768]{2,1,0:T(8,128)(2,1)S(1)}, u32[]{:S(2)}, u32[]{:S(2)}) %collective-permute-start.46) | collective-permute-done | bytes 147488 | tf_op jit(solution)/shard_map/ppermute | solution.py:75
  403.8 7.3 %collective-permute-done.47 = bf16[1,96,768]{2,1,0:T(8,128)(2,1)S(1)} collective-permute-done((bf16[1,96,768]{2,1,0:T(8,128)(2,1)S(1)}, bf16[1,96,768]{2,1,0:T(8,128)(2,1)S(1)}, u32[]{:S(2)}, u32[]{:S(2)}) %collective-permute-start.47) | collective-permute-done | bytes 147488 | tf_op jit(solution)/shard_map/ppermute | solution.py:75
  418.3 8.2 %collective-permute-done.60 = bf16[2,96,768]{2,1,0:T(8,128)(2,1)} collective-permute-done((bf16[2,96,768]{2,1,0:T(8,128)(2,1)}, bf16[2,96,768]{2,1,0:T(8,128)(2,1)}, u32[]{:S(2)}, u32[]{:S(2)}) %collective-permute-start.60) | collective-permute-done | bytes 294944 | tf_op jit(solution)/shard_map/ppermute | solution.py:75
  (718 shorter events, 242.5 us)
Async XLA Ops:
  5.0 48.9 %collective-permute-start.9 = (bf16[2,96,768]{2,1,0:T(8,128)(2,1)}, bf16[2,96,768]{2,1,0:T(8,128)(2,1)}, u32[]{:S(2)}, u32[]{:S(2)}) collective-permute-start(bf16[2,96,768]{2,1,0:T(8,128)(2,1)} %pad_maximum_fusion.4), channel_id=1, source_target_pairs={{0,4},{4,0},{8,12},{12,8},{16,20},{20,16},{24,28},{28,24},{1,5},{5... | collective-permute-start | bytes 884744 | tf_op jit(solution)/shard_map/ppermute | solution.py:71
  7.9 42.2 %collective-permute-start.10 = (bf16[2,96,768]{2,1,0:T(8,128)(2,1)}, bf16[2,96,768]{2,1,0:T(8,128)(2,1)}, u32[]{:S(2)}, u32[]{:S(2)}) collective-permute-start(bf16[2,96,768]{2,1,0:T(8,128)(2,1)} %pad_maximum_fusion.4), channel_id=1, source_target_pairs={{0,8},{4,12},{8,16},{12,20},{16,24},{20,28},{24,0},{28,4},{1,9},{5... | collective-permute-start | bytes 884744 | tf_op jit(solution)/shard_map/ppermute | solution.py:75
  11.7 27.5 %collective-permute-start = (bf16[1,96,768]{1,2,0:T(8,128)(2,1)}, bf16[1,96,768]{1,2,0:T(8,128)(2,1)}, u32[]{:S(2)}, u32[]{:S(2)}) collective-permute-start(bf16[1,96,768]{1,2,0:T(8,128)(2,1)} %get-tuple-element.134), channel_id=1, source_target_pairs={{0,4},{4,0},{8,12},{12,8},{16,20},{20,16},{24,28},{28,24},{1,5},{5... | collective-permute-start | bytes 442376 | tf_op jit(solution)/shard_map/ppermute | solution.py:71
  12.2 28.7 %collective-permute-start.1 = (bf16[1,96,768]{1,2,0:T(8,128)(2,1)}, bf16[1,96,768]{1,2,0:T(8,128)(2,1)}, u32[]{:S(2)}, u32[]{:S(2)}) collective-permute-start(bf16[1,96,768]{1,2,0:T(8,128)(2,1)} %get-tuple-element.134), channel_id=1, source_target_pairs={{0,8},{4,12},{8,16},{12,20},{16,24},{20,28},{24,0},{28,4},{1,9},{5... | collective-permute-start | bytes 442376 | tf_op jit(solution)/shard_map/ppermute | solution.py:75
  50.1 33.6 %collective-permute-start.11 = (bf16[2,96,768]{2,1,0:T(8,128)(2,1)}, bf16[2,96,768]{2,1,0:T(8,128)(2,1)}, u32[]{:S(2)}, u32[]{:S(2)}) collective-permute-start(bf16[2,96,768]{2,1,0:T(8,128)(2,1)} %collective-permute-done.10), channel_id=1, source_target_pairs={{0,4},{4,0},{8,12},{12,8},{16,20},{20,16},{24,28},{28,24},{1,5},{5... | collective-permute-start | bytes 884744 | tf_op jit(solution)/shard_map/ppermute | solution.py:71
  51.6 30.3 %collective-permute-start.12 = (bf16[2,96,768]{2,1,0:T(8,128)(2,1)}, bf16[2,96,768]{2,1,0:T(8,128)(2,1)}, u32[]{:S(2)}, u32[]{:S(2)}) collective-permute-start(bf16[2,96,768]{2,1,0:T(8,128)(2,1)} %collective-permute-done.10), channel_id=1, source_target_pairs={{0,8},{4,12},{8,16},{12,20},{16,24},{20,28},{24,0},{28,4},{1,9},{5... | collective-permute-start | bytes 884744 | tf_op jit(solution)/shard_map/ppermute | solution.py:75
  103.7 21.2 %collective-permute-start.18 = (bf16[1,96,768]{2,1,0:T(8,128)(2,1)S(1)}, bf16[1,96,768]{2,1,0:T(8,128)(2,1)S(1)}, u32[]{:S(2)}, u32[]{:S(2)}) collective-permute-start(bf16[1,96,768]{2,1,0:T(8,128)(2,1)S(1)} %maximum_add_fusion.3), channel_id=1, source_target_pairs={{0,4},{4,0},{8,12},{12,8},{16,20},{20,16},{24,28},{28,24},{1,5},{5... | collective-permute-start | bytes 442376 | tf_op jit(solution)/shard_map/ppermute | solution.py:71
  105.3 18.1 %collective-permute-start.19 = (bf16[1,96,768]{2,1,0:T(8,128)(2,1)S(1)}, bf16[1,96,768]{2,1,0:T(8,128)(2,1)S(1)}, u32[]{:S(2)}, u32[]{:S(2)}) collective-permute-start(bf16[1,96,768]{2,1,0:T(8,128)(2,1)S(1)} %maximum_add_fusion.3), channel_id=1, source_target_pairs={{0,8},{4,12},{8,16},{12,20},{16,24},{20,28},{24,0},{28,4},{1,9},{5... | collective-permute-start | bytes 442376 | tf_op jit(solution)/shard_map/ppermute | solution.py:75
  105.4 30.1 %collective-permute-start.27 = (bf16[2,96,768]{2,1,0:T(8,128)(2,1)S(1)}, bf16[2,96,768]{2,1,0:T(8,128)(2,1)S(1)}, u32[]{:S(2)}, u32[]{:S(2)}) collective-permute-start(bf16[2,96,768]{2,1,0:T(8,128)(2,1)S(1)} %maximum_add_fusion.1), channel_id=1, source_target_pairs={{0,4},{4,0},{8,12},{12,8},{16,20},{20,16},{24,28},{28,24},{1,5},{5... | collective-permute-start | bytes 884744 | tf_op jit(solution)/shard_map/ppermute | solution.py:71
  106.0 27.9 %collective-permute-start.28 = (bf16[2,96,768]{2,1,0:T(8,128)(2,1)S(1)}, bf16[2,96,768]{2,1,0:T(8,128)(2,1)}, u32[]{:S(2)}, u32[]{:S(2)}) collective-permute-start(bf16[2,96,768]{2,1,0:T(8,128)(2,1)S(1)} %maximum_add_fusion.1), channel_id=1, source_target_pairs={{0,8},{4,12},{8,16},{12,20},{16,24},{20,28},{24,0},{28,4},{1,9},{5... | collective-permute-start | bytes 884744 | tf_op jit(solution)/shard_map/ppermute | solution.py:75
  121.5 17.4 %collective-permute-start.16 = (bf16[2,128,768]{2,1,0:T(8,128)(2,1)S(1)}, bf16[2,128,768]{2,1,0:T(8,128)(2,1)S(1)}, u32[]{:S(2)}, u32[]{:S(2)}) collective-permute-start(bf16[2,128,768]{2,1,0:T(8,128)(2,1)S(1)} %fusion.51), channel_id=1, source_target_pairs={{0,1},{1,0},{2,3},{3,2},{4,5},{5,4},{6,7},{7,6},{8,9},{9,8},{10,11... | collective-permute-start | bytes 1179656 | tf_op jit(solution)/shard_map/ppermute | solution.py:71
  133.9 30.9 %collective-permute-start.29 = (bf16[2,96,768]{2,1,0:T(8,128)(2,1)}, bf16[2,96,768]{2,1,0:T(8,128)(2,1)}, u32[]{:S(2)}, u32[]{:S(2)}) collective-permute-start(bf16[2,96,768]{2,1,0:T(8,128)(2,1)} %collective-permute-done.28), channel_id=1, source_target_pairs={{0,4},{4,0},{8,12},{12,8},{16,20},{20,16},{24,28},{28,24},{1,5},{5... | collective-permute-start | bytes 884744 | tf_op jit(solution)/shard_map/ppermute | solution.py:71
  135.4 28.5 %collective-permute-start.30 = (bf16[2,96,768]{2,1,0:T(8,128)(2,1)}, bf16[2,96,768]{2,1,0:T(8,128)(2,1)}, u32[]{:S(2)}, u32[]{:S(2)}) collective-permute-start(bf16[2,96,768]{2,1,0:T(8,128)(2,1)} %collective-permute-done.28), channel_id=1, source_target_pairs={{0,8},{4,12},{8,16},{12,20},{16,24},{20,28},{24,0},{28,4},{1,9},{5... | collective-permute-start | bytes 884744 | tf_op jit(solution)/shard_map/ppermute | solution.py:75
  237.7 44.5 %collective-permute-start.61 = (bf16[2,4,96,768]{3,2,0,1:T(8,128)(2,1)}, bf16[2,4,96,768]{3,2,0,1:T(8,128)(2,1)}, u32[]{:S(2)}, u32[]{:S(2)}) collective-permute-start(bf16[2,4,96,768]{3,2,0,1:T(8,128)(2,1)} %fusion.21), channel_id=1, source_target_pairs={{0,4},{4,0},{8,12},{12,8},{16,20},{20,16},{24,28},{28,24},{1,5},{5... | collective-permute-start | bytes 3538952 | tf_op jit(solution)/shard_map/ppermute | solution.py:71
  265.0 14.5 %collective-permute-start.38 = (bf16[2,128,768]{2,1,0:T(8,128)(2,1)}, bf16[2,128,768]{2,1,0:T(8,128)(2,1)}, u32[]{:S(2)}, u32[]{:S(2)}) collective-permute-start(bf16[2,128,768]{2,1,0:T(8,128)(2,1)} %fusion.55), channel_id=1, source_target_pairs={{0,1},{1,0},{2,3},{3,2},{4,5},{5,4},{6,7},{7,6},{8,9},{9,8},{10,11... | collective-permute-start | bytes 1179656 | tf_op jit(solution)/shard_map/ppermute | solution.py:71
  273.6 25.7 %collective-permute-start.48 = (bf16[1,4,96,768]{3,2,1,0:T(8,128)(2,1)}, bf16[1,4,96,768]{3,2,1,0:T(8,128)(2,1)}, u32[]{:S(2)}, u32[]{:S(2)}) collective-permute-start(bf16[1,4,96,768]{3,2,1,0:T(8,128)(2,1)} %fusion.33), channel_id=1, source_target_pairs={{0,4},{4,0},{8,12},{12,8},{16,20},{20,16},{24,28},{28,24},{1,5},{5... | collective-permute-start | bytes 1769480 | tf_op jit(solution)/shard_map/ppermute | solution.py:71
  284.4 28.6 %collective-permute-start.62 = (bf16[2,96,768]{2,1,0:T(8,128)(2,1)S(1)}, bf16[2,96,768]{2,1,0:T(8,128)(2,1)S(1)}, u32[]{:S(2)}, u32[]{:S(2)}) collective-permute-start(bf16[2,96,768]{2,1,0:T(8,128)(2,1)S(1)} %fusion.82), channel_id=1, source_target_pairs={{0,8},{4,12},{8,16},{12,20},{16,24},{20,28},{24,0},{28,4},{1,9},{5... | collective-permute-start | bytes 884744 | tf_op jit(solution)/shard_map/ppermute | solution.py:75
  311.4 74.6 %collective-permute-start.57 = (bf16[2,4,96,768]{3,2,0,1:T(8,128)(2,1)}, bf16[2,4,96,768]{3,2,0,1:T(8,128)(2,1)}, u32[]{:S(2)}, u32[]{:S(2)}) collective-permute-start(bf16[2,4,96,768]{3,2,0,1:T(8,128)(2,1)} %fusion.20), channel_id=1, source_target_pairs={{0,4},{4,0},{8,12},{12,8},{16,20},{20,16},{24,28},{28,24},{1,5},{5... | collective-permute-start | bytes 3538952 | tf_op jit(solution)/shard_map/ppermute | solution.py:71
  312.7 37.8 %collective-permute-start.50 = (bf16[1,96,768]{2,1,0:T(8,128)(2,1)}, bf16[1,96,768]{2,1,0:T(8,128)(2,1)}, u32[]{:S(2)}, u32[]{:S(2)}) collective-permute-start(bf16[1,96,768]{2,1,0:T(8,128)(2,1)} %fusion.86), channel_id=1, source_target_pairs={{0,8},{4,12},{8,16},{12,20},{16,24},{20,28},{24,0},{28,4},{1,9},{5... | collective-permute-start | bytes 442376 | tf_op jit(solution)/shard_map/ppermute | solution.py:75
  327.7 53.3 %collective-permute-start.64 = (bf16[2,96,768]{2,1,0:T(8,128)(2,1)}, bf16[2,96,768]{2,1,0:T(8,128)(2,1)}, u32[]{:S(2)}, u32[]{:S(2)}) collective-permute-start(bf16[2,96,768]{2,1,0:T(8,128)(2,1)} %fusion.34), channel_id=1, source_target_pairs={{0,8},{4,12},{8,16},{12,20},{16,24},{20,28},{24,0},{28,4},{1,9},{5... | collective-permute-start | bytes 884744 | tf_op jit(solution)/shard_map/ppermute | solution.py:75
  348.8 34.4 %collective-permute-start.42 = (bf16[2,128,768]{2,1,0:T(8,128)(2,1)}, bf16[2,128,768]{2,1,0:T(8,128)(2,1)}, u32[]{:S(2)}, u32[]{:S(2)}) collective-permute-start(bf16[2,128,768]{2,1,0:T(8,128)(2,1)} %fusion.57), channel_id=1, source_target_pairs={{0,1},{1,0},{2,3},{3,2},{4,5},{5,4},{6,7},{7,6},{8,9},{9,8},{10,11... | collective-permute-start | bytes 1179656 | tf_op jit(solution)/shard_map/ppermute | solution.py:71
  352.3 21.7 %collective-permute-start.51 = (bf16[1,96,768]{2,1,0:T(8,128)(2,1)}, bf16[1,96,768]{2,1,0:T(8,128)(2,1)}, u32[]{:S(2)}, u32[]{:S(2)}) collective-permute-start(bf16[1,96,768]{2,1,0:T(8,128)(2,1)} %fusion.85), channel_id=1, source_target_pairs={{0,8},{4,12},{8,16},{12,20},{16,24},{20,28},{24,0},{28,4},{1,9},{5... | collective-permute-start | bytes 442376 | tf_op jit(solution)/shard_map/ppermute | solution.py:75
  371.1 14.7 %collective-permute-start.44 = (bf16[1,4,96,768]{3,2,1,0:T(8,128)(2,1)S(1)}, bf16[1,4,96,768]{3,2,1,0:T(8,128)(2,1)S(1)}, u32[]{:S(2)}, u32[]{:S(2)}) collective-permute-start(bf16[1,4,96,768]{3,2,1,0:T(8,128)(2,1)S(1)} %fusion.32), channel_id=1, source_target_pairs={{0,4},{4,0},{8,12},{12,8},{16,20},{20,16},{24,28},{28,24},{1,5},{5... | collective-permute-start | bytes 1769480 | tf_op jit(solution)/shard_map/ppermute | solution.py:71
  388.0 14.6 %collective-permute-start.58 = (bf16[2,96,768]{2,1,0:T(8,128)(2,1)S(1)}, bf16[2,96,768]{2,1,0:T(8,128)(2,1)S(1)}, u32[]{:S(2)}, u32[]{:S(2)}) collective-permute-start(bf16[2,96,768]{2,1,0:T(8,128)(2,1)S(1)} %fusion.81), channel_id=1, source_target_pairs={{0,8},{4,12},{8,16},{12,20},{16,24},{20,28},{24,0},{28,4},{1,9},{5... | collective-permute-start | bytes 884744 | tf_op jit(solution)/shard_map/ppermute | solution.py:75
  (207 other events, 1550.7 us)
